TPU v7x, 256 devices: a whole 4x4x8 slice. The times are simulated.
256 devices in a mesh: seq: 64 (over z, x, core), head: 4 (over y).
Axes of the slice: x: 4, y: 4, z: 8, core: 2. Of those that a mesh axis runs over, the one named last changes fastest.
Arguments:
- queries: bfloat16 [8704, 1024], P('seq', 'head'), may hold values from -5 to 5
- key_rows: bfloat16 [8704, 1024], P('seq', 'head'), may hold values from -5 to 5
- value_rows: bfloat16 [8704, 1024], P('seq', 'head'), may hold values from -6 to 6
- scale_of: int32 [8704], P('seq'), may hold values from -1 to 12, as said below
- wo: bfloat16 [1024, 2048], P('head'), may hold values from -0.1875 to 0.1875
- dy: bfloat16 [8704, 2048], P('seq', 'head'), may hold values from -16 to 16
Outputs:
- block_out: bfloat16 [8704, 2048], P('seq', 'head')
- dq: bfloat16 [8704, 1024], P('seq', 'head')
- dk: bfloat16 [8704, 1024], P('seq', 'head')
- dv: bfloat16 [8704, 1024], P('seq', 'head')
- dwo: float32 [1024, 2048], P('head', 'seq')
Inputs may be any that keep to these rules, and one draw needn't show every extreme that they name: `scale_of`: in each aligned block of 136 rows (one index of seq) the first 128 rows hold ids 13 - 3 to 12, not falling over these rows of all blocks taken in order, each of the three ids present; the last 8 rows of a block are all -1 except in exactly 4 blocks, whose last rows hold ids 0 to 9, not falling within the block.
All inputs are finite; a program needn't handle non-finite values.
Results may differ from a plain program's by a relative error of at most 0.035.
Values may be sent and summed in bfloat16 or wider, within the bound.
No kernel may reach another device: no remote copies, remote signals or barrier semaphores. Data moves between devices by JAX's collectives and lax.ppermute only.
A program may use at most 192 MiB of HBM per device.

v0:
```python
import functools
import math

import jax
import jax.numpy as jnp
from jax import lax
from jax.experimental import pallas as pl
from jax.experimental.pallas import tpu as pltpu
from jax.sharding import Mesh, PartitionSpec as P

DH = 128
ROWS = 136
PAD = 144
FINE = 128
REST = PAD - FINE
PAIR = 2 * PAD
NH = 4
QHALF = 8
NQ = QHALF * PAD
NK = 2 * NQ
QREST = QHALF * FINE
SUMS = 80
LOAD = PAIR + SUMS
FEATS = 2 * DH
MODEL = 2048
WIDE = MODEL // NH
COLS = 32
BLOCK = 384
BIG = -1e30
SCALE = DH ** (-0.5)
UNIT = SCALE * math.log2(math.e)
F32 = jnp.float32
BF16 = jnp.bfloat16
LAST = (((1,), (1,)), ((), ()))
FIRST = (((0,), (0,)), ((), ()))
PARAMS = pltpu.CompilerParams(vmem_limit_bytes=48 << 20)
VMEM = pl.BlockSpec(memory_space=pltpu.VMEM)
SMEM = pl.BlockSpec(memory_space=pltpu.SMEM)


def shape(dims, kind=BF16):
    return jax.ShapeDtypeStruct(dims, kind)


def call(kernel, name, ins, outs, scratch=(), scalars=0, far=0, flops=0):
    near = len(ins) - scalars - far
    cost = pl.CostEstimate(flops=flops, bytes_accessed=1 << 20, transcendentals=0) if flops else None
    return pl.pallas_call(
        kernel,
        in_specs=[SMEM] * scalars + [pl.BlockSpec(memory_space=pl.ANY)] * far + [VMEM] * near,
        out_shape=outs,
        scratch_shapes=list(scratch),
        compiler_params=PARAMS,
        cost_estimate=cost,
        name=name,
    )(*ins)


def by_parity(e, first, second, keep_ref, send_ref):
    @pl.when(e == 0)
    def _():
        keep_ref[...] = first
        send_ref[...] = second

    @pl.when(e == 1)
    def _():
        keep_ref[...] = second
        send_ref[...] = first


def pack_kernel(at_ref, q_hbm, k_hbm, v_hbm, ids_ref, keep_ref, send_ref, qkeep_ref, qsend_ref, here_ref, sems):
    copies = [
        pltpu.make_async_copy(ref, here_ref.at[i], sems.at[i]) for i, ref in enumerate((q_hbm, k_hbm, v_hbm))
    ]
    for copy in copies:
        copy.start()
    ids = ids_ref[...].astype(BF16)
    zero = jnp.zeros((8, DH), BF16)
    for copy in copies:
        copy.wait()
    kvs, qs = [], []
    for head in range(2):
        cols = slice(head * DH, (head + 1) * DH)
        k = jnp.concatenate([here_ref[1, :, cols], ids], axis=0)
        v = jnp.concatenate([here_ref[2, :, cols], zero], axis=0)
        kvs.append(jnp.concatenate([k, v], axis=1))
        qs.append(jnp.concatenate([here_ref[0, :, cols], ids], axis=0))
    by_parity(at_ref[0], kvs[0], kvs[1], keep_ref, send_ref)
    by_parity(at_ref[0], qs[0], qs[1], qkeep_ref, qsend_ref)


def dattn_kernel(at_ref, dy0_ref, dy1_ref, dy2_ref, dy3_ref, wo_ref, ids_ref, qkeep_ref, qsend_ref, keep_ref, send_ref):
    h = at_ref[1]
    acc = jnp.zeros((ROWS, FEATS), F32)
    for s, ref in enumerate((dy0_ref, dy1_ref, dy2_ref, dy3_ref)):
        start = pl.multiple_of(lax.rem(h - s + NH, NH) * WIDE, WIDE)
        acc = acc + lax.dot_general(ref[...], wo_ref[:, pl.ds(start, WIDE)], LAST, preferred_element_type=F32)
    ids = ids_ref[...].T
    real = jnp.concatenate([ids[:, 0:1], ids[0:8, 1:2]], axis=0) >= 0.0
    acc = jnp.where(real, acc, 0.0).astype(BF16)
    acc = jnp.concatenate([acc, jnp.zeros((PAD - ROWS, FEATS), BF16)], axis=0)
    keep_ref[:, 0:DH] = qkeep_ref[...]
    send_ref[:, 0:DH] = qsend_ref[...]
    by_parity(at_ref[0], acc[:, 0:DH], acc[:, DH:FEATS], keep_ref.at[:, DH:FEATS], send_ref.at[:, DH:FEATS])


def assemble(pair_refs, all_ref, base):
    rest = base + QREST
    for j, ref in enumerate(pair_refs):
        for k in range(2):
            half = 2 * j + k
            all_ref[base + half * FINE : base + (half + 1) * FINE] = ref[k * PAD : k * PAD + FINE]
            all_ref[rest + half * REST : rest + (half + 1) * REST] = ref[k * PAD + FINE : (k + 1) * PAD]


def take_pair(value, j):
    pieces = []
    for half in (2 * j, 2 * j + 1):
        pieces.append(value[half * FINE : (half + 1) * FINE])
        pieces.append(value[QREST + half * REST : QREST + (half + 1) * REST])
    return jnp.concatenate(pieces, axis=0)


def masks(pair_refs, mask_ref, base, is_query):
    fine, last = [], []
    for ref in pair_refs:
        for k in range(2):
            rows = ref[k * PAD + FINE : (k + 1) * PAD, 0:DH].astype(F32)
            fine.append(rows[8:9])
            last.append(rows[9:10])
    fine = jnp.concatenate(fine, axis=0).T
    last = jnp.concatenate(last, axis=0).T
    rest = base + QREST

    def encode(column):
        lane = lax.broadcasted_iota(jnp.int32, (column.shape[0], DH), 1).astype(F32)
        if is_query:
            hidden = ((lane > column) & (lane < 13.0)) | (lane == 13.0)
            return jnp.where(hidden, BIG, 0.0).astype(BF16)
        return jnp.where(lane == jnp.where(column < 0.0, 13.0, column), 1.0, 0.0).astype(BF16)

    for half in range(2 * len(pair_refs)):
        mask_ref[base + half * FINE : base + (half + 1) * FINE] = encode(fine[:, half : half + 1])
        mask_ref[rest + half * REST : rest + (half + 1) * REST] = encode(last[0:REST, half : half + 1])


def in_three(row):
    high = row.astype(BF16).astype(F32)
    middle = (row - high).astype(BF16).astype(F32)
    return [high, middle, row - high - middle]


def forward_kernel(*refs):
    q_parts, kv_parts = refs[0:4], refs[4:12]
    load_refs, q_ref, qm_ref, kv_ref, km_ref, o_ref, stat_ref = refs[12:16], *refs[16:22]
    assemble(q_parts, q_ref, 0)
    masks(q_parts, qm_ref, 0, True)
    for base, parts in ((0, kv_parts[0:4]), (NQ, kv_parts[4:8])):
        assemble(parts, kv_ref, base)
        masks(parts, km_ref, base, False)
    k_ext = jnp.concatenate([kv_ref[:, 0:DH], km_ref[...]], axis=1)
    lane = lax.broadcasted_iota(jnp.int32, (BLOCK, DH), 1)
    for block in range(NQ // BLOCK):
        rows = slice(block * BLOCK, (block + 1) * BLOCK)
        q_ext = jnp.concatenate([q_ref[rows, 0:DH], qm_ref[rows]], axis=1)
        s = lax.dot_general(q_ext, k_ext, LAST, preferred_element_type=F32)
        top = jnp.max(s, axis=1, keepdims=True)
        p = jnp.exp2((s - top) * UNIT)
        total = jnp.sum(p, axis=1, keepdims=True)
        o = jnp.dot(p.astype(BF16), kv_ref[:, DH:FEATS], preferred_element_type=F32) / total
        o_ref[rows] = o.astype(BF16)
        lse = top * UNIT + jnp.log2(total)
        share = jnp.sum(o * q_ref[rows, DH:FEATS].astype(F32), axis=1, keepdims=True)
        stat = jnp.where(lane == 0, lse, jnp.where(lane == 1, share, 0.0))
        stat_ref[:, rows] = stat.T[0:8]
    none = jnp.zeros((2, NQ), F32)
    sums = jnp.concatenate(in_three(stat_ref[0:1]) + in_three(stat_ref[1:2]) + [none], axis=0)
    tiles = [sums[:, i * DH : (i + 1) * DH] for i in range(NQ // DH)] + [jnp.zeros((8, DH), F32)]
    sums = jnp.concatenate(tiles, axis=0).astype(BF16)
    for j in range(4):
        load_refs[j][0:PAIR] = take_pair(o_ref, j)
        load_refs[j][PAIR:LOAD] = sums


def row_sums(load_refs):
    lses, shares = [], []
    for s, ref in enumerate(load_refs):
        sums = ref[PAIR:LOAD].astype(F32)
        tiles = [sums[8 * i : 8 * i + 8] for i in range(9)]
        last = tiles[8] if s == 0 else pltpu.roll(tiles[8], FINE - 2 * REST * s, 1)
        order = [tiles[2 * ((j + s) % 4) + k] for j in range(4) for k in range(2)] + [last]
        rows = jnp.concatenate(order, axis=1)
        lses.append(rows[0:1] + rows[1:2] + rows[2:3])
        shares.append(rows[3:4] + rows[4:5] + rows[5:6])
    top = jnp.maximum(jnp.maximum(lses[0], lses[1]), jnp.maximum(lses[2], lses[3]))
    weights = [jnp.exp2(one - top) for one in lses]
    total = weights[0] + weights[1] + weights[2] + weights[3]
    delta = sum(weights[s] * shares[s] for s in range(4)) / total
    lse = top + jnp.log2(total)
    return jnp.where(lse < -1e28, 1e30, lse), delta


def backward_kernel(base, q_ref, qm_ref, kv_ref, km_ref, *refs):
    load_refs, refs = refs[0:4], refs[4:]
    if base == 0:
        dq_in_ref, refs = refs[0], refs[1:]
    dkv_out_ref, dq_refs, dkv_ref, ds_ref = refs[0], refs[1:-2], refs[-2], refs[-1]
    lse, delta = row_sums(load_refs)
    q = q_ref[:, 0:DH]
    da = q_ref[:, DH:FEATS]
    q_ext = jnp.concatenate([q, qm_ref[...]], axis=1)
    for block in range(NQ // BLOCK):
        rows = slice(block * BLOCK, (block + 1) * BLOCK)
        keys = slice(base + block * BLOCK, base + (block + 1) * BLOCK)
        k_ext = jnp.concatenate([kv_ref[keys, 0:DH], km_ref[keys]], axis=1)
        s = lax.dot_general(k_ext, q_ext, LAST, preferred_element_type=F32)
        p = jnp.exp2(s * UNIT - lse)
        dp = lax.dot_general(kv_ref[keys, DH:FEATS], da, LAST, preferred_element_type=F32)
        ds = (p * (dp - delta)).astype(BF16)
        dkv_ref[rows, DH:FEATS] = jnp.dot(p.astype(BF16), da, preferred_element_type=F32).astype(BF16)
        dkv_ref[rows, 0:DH] = (jnp.dot(ds, q, preferred_element_type=F32) * SCALE).astype(BF16)
        ds_ref[rows] = ds
    for j in range(4):
        dkv_out_ref[j] = take_pair(dkv_ref, j)
    keys = slice(base, base + NQ)
    dq = lax.dot_general(ds_ref[...], kv_ref[keys, 0:DH], FIRST, preferred_element_type=F32)
    if base > 0:
        dq_refs[0][...] = dq
    else:
        dq = ((dq + dq_in_ref[...]) * SCALE).astype(BF16)
        for j in range(4):
            dq_refs[j][...] = take_pair(dq, j)


def merge_kernel(l0_ref, l1_ref, l2_ref, l3_ref, keep_ref, send_ref):
    load_refs = (l0_ref, l1_ref, l2_ref, l3_ref)
    fine, last = [], []
    for s, ref in enumerate(load_refs):
        sums = ref[PAIR:LOAD].astype(F32)
        rows = sums[0:72]
        lse = [rows[8 * i : 8 * i + 1] + rows[8 * i + 1 : 8 * i + 2] + rows[8 * i + 2 : 8 * i + 3] for i in (2 * s, 2 * s + 1, 8)]
        fine += lse[0:2]
        last.append(lse[2] if s == 0 else pltpu.roll(lse[2], FINE - 2 * REST * s, 1))
    fine = jnp.concatenate(fine, axis=0).T
    last = jnp.concatenate(last + last, axis=0).T
    for k, out_ref in ((0, keep_ref), (1, send_ref)):
        for rows, columns in (
            (slice(0, FINE), [fine[:, 2 * s + k : 2 * s + k + 1] for s in range(4)]),
            (slice(FINE, PAD), [last[k * REST : (k + 1) * REST, s : s + 1] for s in range(4)]),
        ):
            source = slice(k * PAD + rows.start, k * PAD + rows.stop)
            top = jnp.maximum(jnp.maximum(columns[0], columns[1]), jnp.maximum(columns[2], columns[3]))
            weights = [jnp.exp2(one - top) for one in columns]
            total = weights[0] + weights[1] + weights[2] + weights[3]
            acc = sum(weights[s] * load_refs[s][source].astype(F32) for s in range(4))
            out_ref[rows] = (acc * jnp.where(top < -1e28, 0.0, 1.0 / total)).astype(BF16)


def project_kernel(at_ref, mine_ref, other_ref, wo_ref, dy0_ref, dy1_ref, dy2_ref, dy3_ref, *refs):
    out_refs, keep_ref, send_ref, dwo_ref = refs[0:4], *refs[4:7]
    e, h, zr, x, c = (at_ref[i] for i in range(5))
    mine, other = mine_ref[...], other_ref[...]
    even = e == 0
    attn = jnp.concatenate([jnp.where(even, mine, other), jnp.where(even, other, mine)], axis=1)
    for s in range(NH):
        start = pl.multiple_of(lax.rem(h + s, NH) * WIDE, WIDE)
        part = jnp.dot(attn, wo_ref[:, pl.ds(start, WIDE)], preferred_element_type=F32)
        out_refs[s][...] = part[0:ROWS].astype(BF16)
    for s, ref in enumerate((dy0_ref, dy1_ref, dy2_ref, dy3_ref)):
        dwo_ref[s] = lax.dot_general(ref[...], attn[0:ROWS], FIRST, preferred_element_type=F32).astype(BF16)
    for xt in range(4):
        for et in range(2):
            for t in range(4):
                s = lax.rem(h - jnp.bitwise_xor(zr, t) + NH, NH)
                row = lax.rem(e + et, 2) * 256 + lax.rem(x + xt, 4) * 64
                to = slice((et * 4 + t) * COLS, (et * 4 + t + 1) * COLS)
                keep_ref[xt, to] = dwo_ref[s, pl.ds(pl.multiple_of(row + c * COLS, COLS), COLS)]
                send_ref[xt, to] = dwo_ref[s, pl.ds(pl.multiple_of(row + (1 - c) * COLS, COLS), COLS)]


def core_kernel(keep_ref, got_ref, wkeep_ref, wgot_ref, dq1_ref, dq2_ref, dq3_ref, *refs):
    mine_ref, z_refs, wmine_ref, x_refs = refs[0], refs[1:4], refs[4], refs[5:8]
    total = keep_ref[...].astype(F32) + got_ref[...].astype(F32)
    mine_ref[...] = total[0]
    weights = wkeep_ref[...].astype(F32) + wgot_ref[...].astype(F32)
    wmine_ref[...] = weights[0]
    for s, dq_ref in ((1, dq1_ref), (2, dq2_ref), (3, dq3_ref)):
        z_refs[s - 1][...] = total[s].astype(BF16)
        piece = weights[4 - s].astype(BF16)
        x_refs[s - 1][0:PAIR] = dq_ref[...]
        x_refs[s - 1][PAIR : PAIR + 256] = piece[:, 0:DH]
        x_refs[s - 1][PAIR + 256 : PAIR + 512] = piece[:, DH:FEATS]


def ring_kernel(dq0_ref, wmine_ref, x1_ref, x2_ref, x3_ref, dq_ref, keep_ref, send_ref):
    got = [ref[...].astype(F32) for ref in (x1_ref, x2_ref, x3_ref)]
    got = got[0] + got[1] + got[2]
    dq_ref[...] = dq0_ref[...].astype(F32) + got[0:PAIR]
    total = wmine_ref[...] + jnp.concatenate([got[PAIR : PAIR + 256], got[PAIR + 256 : PAIR + 512]], axis=1)
    for et in range(2):
        at = et * 4 * COLS
        to = et * 2 * COLS
        keep_ref[to : to + 2 * COLS] = total[at : at + 2 * COLS]
        send_ref[to : to + COLS] = total[at + 3 * COLS : at + 4 * COLS].astype(BF16)
        send_ref[to + COLS : to + 2 * COLS] = total[at + 2 * COLS : at + 3 * COLS].astype(BF16)


def half_kernel(keep_ref, got_ref, out_ref, send_ref):
    total = keep_ref[...] + got_ref[...].astype(F32)
    for et in range(2):
        out_ref[et * COLS : (et + 1) * COLS] = total[et * 2 * COLS : (et * 2 + 1) * COLS]
        send_ref[et * COLS : (et + 1) * COLS] = total[(et * 2 + 1) * COLS : (et * 2 + 2) * COLS].astype(BF16)


def total_kernel(k0_ref, k1_ref, k2_ref, k3_ref, dq_ref, wkeep_ref, wgot_ref, keep_ref, wmine_ref, send_ref):
    dkv = k0_ref[...] + sum(ref[...].astype(F32) for ref in (k1_ref, k2_ref, k3_ref))
    both = jnp.concatenate([dq_ref[...], dkv], axis=1).astype(BF16)
    keep_ref[...] = both[0:PAD]
    for i in range(3):
        send_ref[i * PAD : (i + 1) * PAD] = both[PAD:PAIR, i * DH : (i + 1) * DH]
    weights = wkeep_ref[...] + wgot_ref[...].astype(F32)
    wmine_ref[...] = weights[0:COLS]
    piece = weights[COLS : 2 * COLS].astype(BF16)
    send_ref[3 * PAD : 3 * PAD + COLS] = piece[:, 0:DH]
    send_ref[3 * PAD + COLS : 3 * PAD + 2 * COLS] = piece[:, DH:FEATS]


def place_kernel(at_ref, mine_ref, wmine_ref, got_ref, dq_ref, dk_ref, dv_ref, dwo_ref):
    even = at_ref[0] == 0
    for i, ref in enumerate((dq_ref, dk_ref, dv_ref)):
        mine = mine_ref[0:ROWS, i * DH : (i + 1) * DH]
        other = got_ref[i * PAD : i * PAD + ROWS]
        ref[:, 0:DH] = jnp.where(even, mine, other)
        ref[:, DH:FEATS] = jnp.where(even, other, mine)
    got = got_ref[3 * PAD : 3 * PAD + 2 * COLS].astype(F32)
    dwo_ref[...] = (wmine_ref[...] + jnp.concatenate([got[0:COLS], got[COLS : 2 * COLS]], axis=1)).T


def shifted(value, axis, size, by):
    return lax.ppermute(value, axis, [(i, (i + by) % size) for i in range(size)])


def swapped(value, axis, size, mask):
    return lax.ppermute(value, axis, [(i, i ^ mask) for i in range(size)])


def around(value, axis):
    return [value] + [shifted(value, axis, 4, s) for s in (1, 2, 3)]


def local(queries, key_rows, value_rows, scale_of, wo, dy):
    axes = ("e", "head", "zr", "x", "c")
    at = jnp.stack([lax.axis_index(name) for name in axes]).astype(jnp.int32)
    ids = jnp.pad(scale_of, (0, 8 * DH - ROWS), constant_values=-1).reshape(8, DH).astype(F32)
    pair = (PAIR, FEATS)

    keep, send, qkeep, qsend = call(
        pack_kernel,
        "pack",
        [at, queries, key_rows, value_rows, ids],
        [shape((PAD, FEATS))] * 2 + [shape((PAD, DH))] * 2,
        [pltpu.VMEM((3, ROWS, FEATS), BF16), pltpu.SemaphoreType.DMA((3,))],
        scalars=1,
        far=3,
    )
    kvs = around(jnp.concatenate([keep, swapped(send, "e", 2, 1)], axis=0), "zr")
    dys = around(dy, "head")
    keep, send = call(
        dattn_kernel, "dattn", [at, *dys, wo, ids, qkeep, qsend], [shape((PAD, FEATS))] * 2, scalars=1
    )
    qs = around(jnp.concatenate([keep, swapped(send, "e", 2, 1)], axis=0), "x")
    kvs = kvs + [swapped(one, "c", 2, 1) for one in kvs]

    *loads, q, qm, kv, km = call(
        forward_kernel,
        "forward",
        [*qs, *kvs],
        [shape((LOAD, DH))] * 4 + [shape((NQ, FEATS)), shape((NQ, DH)), shape((NK, FEATS)), shape((NK, DH))],
        [pltpu.VMEM((NQ, DH), BF16), pltpu.VMEM((8, NQ), F32)],
        flops=6 * NQ * NK * DH,
    )
    loads = [loads[0]] + [shifted(loads[s], "x", 4, -s) for s in (1, 2, 3)]

    keep, send = call(merge_kernel, "merge", loads, [shape((PAD, DH))] * 2)
    other = swapped(send, "e", 2, 1)
    scratch = [pltpu.VMEM((NQ, FEATS), BF16), pltpu.VMEM((NQ, NQ), BF16)]
    dkv_send, dq_part = call(
        functools.partial(backward_kernel, NQ),
        "backward_far",
        [q, qm, kv, km, *loads],
        [shape((4, *pair)), shape((NQ, DH), F32)],
        scratch,
        flops=6 * NQ * NK * DH,
    )
    other, dq_part = lax.optimization_barrier((other, dq_part))
    *outs, wkeep, wsend = call(
        project_kernel,
        "project",
        [at, keep, other, wo, *dys],
        [shape((ROWS, WIDE))] * 4 + [shape((4, 256, FEATS))] * 2,
        [pltpu.VMEM((4, WIDE, FEATS), BF16)],
        scalars=1,
    )
    wsend, dq_part = lax.optimization_barrier((wsend, dq_part))
    dkv_keep, *dqs = call(
        functools.partial(backward_kernel, 0),
        "backward_near",
        [q, qm, kv, km, *loads, dq_part],
        [shape((4, *pair))] + [shape((PAIR, DH))] * 4,
        scratch,
        flops=6 * NQ * NK * DH,
    )
    mine, *far = call(
        core_kernel,
        "core",
        [dkv_keep, swapped(dkv_send, "c", 2, 1), wkeep, swapped(wsend, "c", 2, 1), *dqs[1:]],
        [shape(pair, F32)] + [shape(pair)] * 3 + [shape((256, FEATS), F32)] + [shape((PAIR + 512, DH))] * 3,
    )
    dkvs = [mine] + [shifted(far[s - 1], "zr", 4, -s) for s in (1, 2, 3)]
    xs = [shifted(far[3 + s], "x", 4, -s) for s in (1, 2, 3)]
    dq, wkeep, wsend = call(
        ring_kernel,
        "ring",
        [dqs[0], far[3], *xs],
        [shape((PAIR, DH), F32), shape((128, FEATS), F32), shape((128, FEATS))],
    )
    wkeep, wsend = call(
        half_kernel,
        "half",
        [wkeep, swapped(wsend, "zr", 4, 3)],
        [shape((64, FEATS), F32), shape((64, FEATS))],
    )
    block_out = sum(
        [outs[0].astype(F32)] + [shifted(outs[s], "head", NH, s).astype(F32) for s in (1, 2, 3)]
    ).astype(BF16)
    keep, wkeep, send = call(
        total_kernel,
        "total",
        [*dkvs, dq, wkeep, swapped(wsend, "zr", 4, 1)],
        [shape((PAD, 3 * DH)), shape((COLS, FEATS), F32), shape((3 * PAD + 2 * COLS, DH))],
    )
    dq, dk, dv, dwo = call(
        place_kernel,
        "place",
        [at, keep, wkeep, swapped(send, "e", 2, 1)],
        [shape((ROWS, FEATS))] * 3 + [shape((FEATS, COLS), F32)],
        scalars=1,
    )
    return (block_out, dq, dk, dv, dwo)


def solution(mesh):
    fine = Mesh(mesh.devices.reshape(4, 2, 4, 2, NH), ("zr", "e", "x", "c", "head"))
    seq = ("zr", "e", "x", "c")
    placed = (
        P(seq, "head"),
        P(seq, "head"),
        P(seq, "head"),
        P(seq),
        P("head", None),
        P(seq, "head"),
    )
    return jax.shard_map(
        local,
        mesh=fine,
        in_specs=placed,
        out_specs=(
            P(seq, "head"),
            P(seq, "head"),
            P(seq, "head"),
            P(seq, "head"),
            P("head", seq),
        ),
        check_vma=False,
    )
```

profile of v0, /device:TPU:8, one launch (start us, length us, event | category | flops | bytes accessed | tf_op | source)
XLA Modules:
  0.0 119.3 jit_solution(13549896296480512622)
XLA Ops:
  0.6 1.7 %collective-permute-start = (bf16[136,512]{1,0:T(8,128)(2,1)}, bf16[136,512]{1,0:T(8,128)(2,1)S(1)}, u32[]{:S(2)}, u32[]{:S(2)}) collective-permute-start(bf16[136,512]{1,0:T(8,128)(2,1)} %dy0_ref.3), channel_id=1, source_target_pairs={{0,1},{1,2},{2,3},{3,0},{4,5},{5,6},{6,7},{7,4},{8,9},{9,10},{10,1... | collective-permute-start | bytes 417800 | tf_op jit(solution)/shard_map/ppermute | solution.py:340
  2.3 2.7 %collective-permute-start.1 = (bf16[136,512]{1,0:T(8,128)(2,1)}, bf16[136,512]{1,0:T(8,128)(2,1)S(1)}, u32[]{:S(2)}, u32[]{:S(2)}) collective-permute-start(bf16[136,512]{1,0:T(8,128)(2,1)} %dy0_ref.3), channel_id=1, source_target_pairs={{0,2},{1,3},{2,0},{3,1},{4,6},{5,7},{6,4},{7,5},{8,10},{9,11},{10,... | collective-permute-start | bytes 417800 | tf_op jit(solution)/shard_map/ppermute | solution.py:340
  5.0 0.7 collective-permute-start.2
  5.6 0.7 convert_bitcast_fusion.ids_ref
  6.3 0.1 stack.23.at_ref
  6.4 0.9 copy-done.4
  7.3 0.9 copy-done.5
  8.2 0.9 copy-done.6
  9.1 0.9 pack.1
  10.0 2.0 %collective-permute-start.7 = (bf16[144,256]{1,0:T(8,128)(2,1)S(1)}, bf16[144,256]{1,0:T(8,128)(2,1)S(1)}, u32[]{:S(2)}, u32[]{:S(2)}) collective-permute-start(bf16[144,256]{1,0:T(8,128)(2,1)S(1)} %get-tuple-element.63), channel_id=1, source_target_pairs={{0,32},{32,0},{1,33},{33,1},{2,34},{34,2},{3,35},{35,3},{4,36},{36... | collective-permute-start | bytes 221192 | tf_op jit(solution)/shard_map/ppermute | solution.py:344
  12.0 2.4 %collective-permute-done.7 = bf16[144,256]{1,0:T(8,128)(2,1)S(1)} collective-permute-done((bf16[144,256]{1,0:T(8,128)(2,1)S(1)}, bf16[144,256]{1,0:T(8,128)(2,1)S(1)}, u32[]{:S(2)}, u32[]{:S(2)}) %collective-permute-start.7) | collective-permute-done | bytes 73760 | tf_op jit(solution)/shard_map/ppermute | solution.py:344
  14.4 3.3 %collective-permute-start.8 = (bf16[288,256]{1,0:T(8,128)(2,1)S(1)}, bf16[288,256]{1,0:T(8,128)(2,1)S(1)}, u32[]{:S(2)}, u32[]{:S(2)}) collective-permute-start(bf16[288,256]{1,0:T(8,128)(2,1)S(1)} %constant_dynamic-update-slice_fusion.2.refs_4_), channel_id=1, source_target_pairs={{0,64},{64,128},{128,192},{192,0},{1,65},{65,129},{129,193},{193,1... | collective-permute-start | bytes 442376 | tf_op jit(solution)/shard_map/ppermute | solution.py:340
  17.7 5.4 %collective-permute-start.9 = (bf16[288,256]{1,0:T(8,128)(2,1)S(1)}, bf16[288,256]{1,0:T(8,128)(2,1)S(1)}, u32[]{:S(2)}, u32[]{:S(2)}) collective-permute-start(bf16[288,256]{1,0:T(8,128)(2,1)S(1)} %constant_dynamic-update-slice_fusion.2.refs_4_), channel_id=1, source_target_pairs={{0,128},{64,192},{128,0},{192,64},{1,129},{65,193},{129,1},{193,65... | collective-permute-start | bytes 442376 | tf_op jit(solution)/shard_map/ppermute | solution.py:340
  23.1 2.7 %collective-permute-start.10 = (bf16[288,256]{1,0:T(8,128)(2,1)S(1)}, bf16[288,256]{1,0:T(8,128)(2,1)S(1)}, u32[]{:S(2)}, u32[]{:S(2)}) collective-permute-start(bf16[288,256]{1,0:T(8,128)(2,1)S(1)} %constant_dynamic-update-slice_fusion.2.refs_4_), channel_id=1, source_target_pairs={{0,192},{64,0},{128,64},{192,128},{1,193},{65,1},{129,65},{193,129... | collective-permute-start | bytes 442376 | tf_op jit(solution)/shard_map/ppermute | solution.py:340
  25.8 1.2 %copy-done = bf16[256,2048]{1,0:T(8,128)(2,1)S(1)} copy-done((bf16[256,2048]{1,0:T(8,128)(2,1)S(1)}, bf16[256,2048]{1,0:T(8,128)(2,1)}, u32[]{:S(2)}) %copy-start) | copy-done | bytes 1048600
  27.0 0.9 copy-done.2
  27.9 1.0 dattn.1
  28.9 1.1 collective-permute-start.3
  30.1 6.2 %collective-permute-done.3 = bf16[144,256]{1,0:T(8,128)(2,1)S(1)} collective-permute-done((bf16[144,256]{1,0:T(8,128)(2,1)S(1)}, bf16[144,256]{1,0:T(8,128)(2,1)S(1)}, u32[]{:S(2)}, u32[]{:S(2)}) %collective-permute-start.3) | collective-permute-done | bytes 73760 | tf_op jit(solution)/shard_map/ppermute | solution.py:344
  36.3 1.5 %collective-permute-start.4 = (bf16[288,256]{1,0:T(8,128)(2,1)S(1)}, bf16[288,256]{1,0:T(8,128)(2,1)S(1)}, u32[]{:S(2)}, u32[]{:S(2)}) collective-permute-start(bf16[288,256]{1,0:T(8,128)(2,1)S(1)} %constant_dynamic-update-slice_fusion.refs_0_), channel_id=1, source_target_pairs={{0,8},{8,16},{16,24},{24,0},{1,9},{9,17},{17,25},{25,1},{2,10},{10... | collective-permute-start | bytes 442376 | tf_op jit(solution)/shard_map/ppermute | solution.py:340
  37.7 2.7 %collective-permute-start.5 = (bf16[288,256]{1,0:T(8,128)(2,1)S(1)}, bf16[288,256]{1,0:T(8,128)(2,1)S(1)}, u32[]{:S(2)}, u32[]{:S(2)}) collective-permute-start(bf16[288,256]{1,0:T(8,128)(2,1)S(1)} %constant_dynamic-update-slice_fusion.refs_0_), channel_id=1, source_target_pairs={{0,16},{8,24},{16,0},{24,8},{1,17},{9,25},{17,1},{25,9},{2,18},{10... | collective-permute-start | bytes 442376 | tf_op jit(solution)/shard_map/ppermute | solution.py:340
  40.5 1.4 %collective-permute-start.6 = (bf16[288,256]{1,0:T(8,128)(2,1)S(1)}, bf16[288,256]{1,0:T(8,128)(2,1)S(1)}, u32[]{:S(2)}, u32[]{:S(2)}) collective-permute-start(bf16[288,256]{1,0:T(8,128)(2,1)S(1)} %constant_dynamic-update-slice_fusion.refs_0_), channel_id=1, source_target_pairs={{0,24},{8,0},{16,8},{24,16},{1,25},{9,1},{17,9},{25,17},{2,26},{10... | collective-permute-start | bytes 442376 | tf_op jit(solution)/shard_map/ppermute | solution.py:340
  41.9 0.5 collective-permute-start.13
  42.4 1.8 %collective-permute-done.4.refs_1_ = bf16[288,256]{1,0:T(8,128)(2,1)S(1)} collective-permute-done((bf16[288,256]{1,0:T(8,128)(2,1)S(1)}, bf16[288,256]{1,0:T(8,128)(2,1)S(1)}, u32[]{:S(2)}, u32[]{:S(2)}) %collective-permute-start.4) | collective-permute-done | bytes 147488 | tf_op jit(solution)/shard_map/ppermute | solution.py:340
  44.2 1.8 %collective-permute-done.5.refs_2_ = bf16[288,256]{1,0:T(8,128)(2,1)S(1)} collective-permute-done((bf16[288,256]{1,0:T(8,128)(2,1)S(1)}, bf16[288,256]{1,0:T(8,128)(2,1)S(1)}, u32[]{:S(2)}, u32[]{:S(2)}) %collective-permute-start.5) | collective-permute-done | bytes 147488 | tf_op jit(solution)/shard_map/ppermute | solution.py:340
  46.0 5.0 %forward.1 = (bf16[368,128]{1,0:T(8,128)(2,1)S(1)}, bf16[368,128]{1,0:T(8,128)(2,1)S(1)}, bf16[368,128]{1,0:T(8,128)(2,1)S(1)}, bf16[368,128]{1,0:T(8,128)(2,1)S...) custom-call(bf16[288,256]{1,0:T(8,128)(2,1)S(1)} %constant_dynamic-u, ...), custom_call_target="tpu_custom_call" | custom-call | flops 2038431744 | bytes 1048576 | tf_op jit(solution)/shard_map/forward/pallas_call | solution.py:48
  51.0 2.6 %collective-permute-start.15 = (bf16[368,128]{1,0:T(8,128)(2,1)S(1)}, bf16[368,128]{1,0:T(8,128)(2,1)S(1)}, u32[]{:S(2)}, u32[]{:S(2)}) collective-permute-start(bf16[368,128]{1,0:T(8,128)(2,1)S(1)} %get-tuple-element.65), channel_id=1, source_target_pairs={{0,24},{8,0},{16,8},{24,16},{1,25},{9,1},{17,9},{25,17},{2,26},{10... | collective-permute-start | bytes 282632 | tf_op jit(solution)/shard_map/ppermute | solution.py:340
  53.7 0.9 collective-permute-start.16
  54.5 0.7 collective-permute-start.17
  55.2 1.2 %collective-permute-done.15.l1_ref.refs_1_ = bf16[368,128]{1,0:T(8,128)(2,1)S(1)} collective-permute-done((bf16[368,128]{1,0:T(8,128)(2,1)S(1)}, bf16[368,128]{1,0:T(8,128)(2,1)S(1)}, u32[]{:S(2)}, u32[]{:S(2)}) %collective-permute-start.15) | collective-permute-done | bytes 94240 | tf_op jit(solution)/shard_map/ppermute | solution.py:340
  56.4 3.4 %collective-permute-done.16.l2_ref.refs_2_ = bf16[368,128]{1,0:T(8,128)(2,1)S(1)} collective-permute-done((bf16[368,128]{1,0:T(8,128)(2,1)S(1)}, bf16[368,128]{1,0:T(8,128)(2,1)S(1)}, u32[]{:S(2)}, u32[]{:S(2)}) %collective-permute-start.16) | collective-permute-done | bytes 94240 | tf_op jit(solution)/shard_map/ppermute | solution.py:340
  59.8 1.0 collective-permute-done.17.l3_ref.refs_3_
  60.8 4.1 %backward_far.1 = (bf16[4,288,256]{2,1,0:T(8,128)(2,1)S(1)}, f32[1152,128]{1,0:T(8,128)S(1)}) custom-call(bf16[1152,256]{1,0:T(8,128)(2,1)S(1)} %get-tuple-element.70.q_ref, bf16[1152,128]{1,0:T(8,128)(2,1)S(1)} %get-tuple-element.71.qm_ref, bf16[2304,256]{1,0:T(8,128)(2,1)S(1)} %get-tuple-element.72.kv_ref, bf16[2304,128]{1,0:T(8,128)(2,1)S(1)} %get-tuple-element.73.km_ref, ...), custom_call_target="tpu_custom_call" | custom-call | flops 2038431744 | bytes 1048576 | tf_op jit(solution)/shard_map/backward_far/pallas_call | solution.py:48
  64.9 0.1 collective-permute-start.22
  65.0 0.8 merge.1
  65.8 1.2 collective-permute-start.18
  67.0 3.1 %collective-permute-done.18.other_ref = bf16[144,128]{1,0:T(8,128)(2,1)S(1)} collective-permute-done((bf16[144,128]{1,0:T(8,128)(2,1)S(1)}, bf16[144,128]{1,0:T(8,128)(2,1)S(1)}, u32[]{:S(2)}, u32[]{:S(2)}) %collective-permute-start.18) | collective-permute-done | bytes 36896 | tf_op jit(solution)/shard_map/ppermute | solution.py:344
  70.1 1.3 %project.1 = (bf16[136,512]{1,0:T(8,128)(2,1)S(1)}, bf16[136,512]{1,0:T(8,128)(2,1)S(1)}, bf16[136,512]{1,0:T(8,128)(2,1)S(1)}, bf16[136,512]{1,0:T(8,128)(2,1)S...) custom-call(s32[5]{0:T(128)S(1)} %stack.23.at_ref, ...), custom_call_target="tpu_custom_call" | custom-call | tf_op jit(solution)/shard_map/project/pallas_call | solution.py:48
  71.4 0.1 collective-permute-start.23
  71.5 4.1 %backward_near.1 = (bf16[4,288,256]{2,1,0:T(8,128)(2,1)S(1)}, bf16[288,128]{1,0:T(8,128)(2,1)S(1)}, bf16[288,128]{1,0:T(8,128)(2,1)S(1)}, bf16[288,128]{1,0:T(8,128)(2,1)S(1)}, bf16[288,128]{1,0:T(8,128)(2,1)S(1)}) custom-call(bf16[1152,256]{1,0:T(8,128)(2,1)S(1)} %get-tuple-element.70.q_ref, bf16[1152,128]{1,0:T(8,128)(2,1)S(1)} %get-tuple-element.71.qm_ref, ...), custom_call_target="tpu_custom_call" | custom-call | flops 2038431744 | bytes 1048576 | tf_op jit(solution)/shard_map/backward_near/pallas_call | solution.py:48
  75.6 0.3 core.1
  75.9 0.6 collective-permute-start.27
  76.5 0.9 collective-permute-start.28
  77.4 1.0 collective-permute-start.29
  78.4 2.7 %collective-permute-start.24 = (bf16[288,256]{1,0:T(8,128)(2,1)S(1)}, bf16[288,256]{1,0:T(8,128)(2,1)S(1)}, u32[]{:S(2)}, u32[]{:S(2)}) collective-permute-start(bf16[288,256]{1,0:T(8,128)(2,1)S(1)} %get-tuple-element.91), channel_id=1, source_target_pairs={{0,192},{64,0},{128,64},{192,128},{1,193},{65,1},{129,65},{193,129... | collective-permute-start | bytes 442376 | tf_op jit(solution)/shard_map/ppermute | solution.py:340
  81.1 2.7 %collective-permute-done.27.x1_ref = bf16[800,128]{1,0:T(8,128)(2,1)S(1)} collective-permute-done((bf16[800,128]{1,0:T(8,128)(2,1)S(1)}, bf16[800,128]{1,0:T(8,128)(2,1)S(1)}, u32[]{:S(2)}, u32[]{:S(2)}) %collective-permute-start.27) | collective-permute-done | bytes 204832 | tf_op jit(solution)/shard_map/ppermute | solution.py:340
  83.8 2.2 %collective-permute-done.28.x2_ref = bf16[800,128]{1,0:T(8,128)(2,1)S(1)} collective-permute-done((bf16[800,128]{1,0:T(8,128)(2,1)S(1)}, bf16[800,128]{1,0:T(8,128)(2,1)S(1)}, u32[]{:S(2)}, u32[]{:S(2)}) %collective-permute-start.28) | collective-permute-done | bytes 204832 | tf_op jit(solution)/shard_map/ppermute | solution.py:340
  86.0 3.6 %collective-permute-done.29.x3_ref = bf16[800,128]{1,0:T(8,128)(2,1)S(1)} collective-permute-done((bf16[800,128]{1,0:T(8,128)(2,1)S(1)}, bf16[800,128]{1,0:T(8,128)(2,1)S(1)}, u32[]{:S(2)}, u32[]{:S(2)}) %collective-permute-start.29) | collective-permute-done | bytes 204832 | tf_op jit(solution)/shard_map/ppermute | solution.py:340
  89.6 0.1 ring.1
  89.7 2.8 %collective-permute-start.30 = (bf16[128,256]{1,0:T(8,128)(2,1)S(1)}, bf16[128,256]{1,0:T(8,128)(2,1)S(1)}, u32[]{:S(2)}, u32[]{:S(2)}) collective-permute-start(bf16[128,256]{1,0:T(8,128)(2,1)S(1)} %get-tuple-element.101), channel_id=1, source_target_pairs={{0,192},{64,128},{128,64},{192,0},{1,193},{65,129},{129,65},{193,1... | collective-permute-start | bytes 196616 | tf_op jit(solution)/shard_map/ppermute | solution.py:344
  92.5 1.2 collective-permute-start.25
  93.7 2.6 %collective-permute-start.26 = (bf16[288,256]{1,0:T(8,128)(2,1)S(1)}, bf16[288,256]{1,0:T(8,128)(2,1)S(1)}, u32[]{:S(2)}, u32[]{:S(2)}) collective-permute-start(bf16[288,256]{1,0:T(8,128)(2,1)S(1)} %get-tuple-element.93), channel_id=1, source_target_pairs={{0,64},{64,128},{128,192},{192,0},{1,65},{65,129},{129,193},{193,1... | collective-permute-start | bytes 442376 | tf_op jit(solution)/shard_map/ppermute | solution.py:340
  96.3 1.4 %collective-permute-start.21 = (bf16[136,512]{1,0:T(8,128)(2,1)S(1)}, bf16[136,512]{1,0:T(8,128)(2,1)S(1)}, u32[]{:S(2)}, u32[]{:S(2)}) collective-permute-start(bf16[136,512]{1,0:T(8,128)(2,1)S(1)} %get-tuple-element.79), channel_id=1, source_target_pairs={{0,3},{1,0},{2,1},{3,2},{4,7},{5,4},{6,5},{7,6},{8,11},{9,8},{10,9... | collective-permute-start | bytes 417800 | tf_op jit(solution)/shard_map/ppermute | solution.py:340
  97.7 2.8 %collective-permute-done.30.got_ref = bf16[128,256]{1,0:T(8,128)(2,1)S(1)} collective-permute-done((bf16[128,256]{1,0:T(8,128)(2,1)S(1)}, bf16[128,256]{1,0:T(8,128)(2,1)S(1)}, u32[]{:S(2)}, u32[]{:S(2)}) %collective-permute-start.30) | collective-permute-done | bytes 65568 | tf_op jit(solution)/shard_map/ppermute | solution.py:344
  100.5 0.4 collective-permute-start.19
  100.9 6.4 %collective-permute-done.25.k2_ref = bf16[288,256]{1,0:T(8,128)(2,1)S(1)} collective-permute-done((bf16[288,256]{1,0:T(8,128)(2,1)S(1)}, bf16[288,256]{1,0:T(8,128)(2,1)S(1)}, u32[]{:S(2)}, u32[]{:S(2)}) %collective-permute-start.25) | collective-permute-done | bytes 147488 | tf_op jit(solution)/shard_map/ppermute | solution.py:340
  107.3 0.1 collective-permute-done.26.k3_ref
  107.4 4.8 %collective-permute-done.31.wgot_ref = bf16[64,256]{1,0:T(8,128)(2,1)S(1)} collective-permute-done((bf16[64,256]{1,0:T(8,128)(2,1)S(1)}, bf16[64,256]{1,0:T(8,128)(2,1)S(1)}, u32[]{:S(2)}, u32[]{:S(2)}) %collective-permute-start.31) | collective-permute-done | bytes 32800 | tf_op jit(solution)/shard_map/ppermute | solution.py:344
  112.3 0.1 total.1
  112.3 0.1 collective-permute-start.32
  112.5 0.7 add_convert_fusion
  113.2 4.1 %collective-permute-done.32.got_ref = bf16[496,128]{1,0:T(8,128)(2,1)S(1)} collective-permute-done((bf16[496,128]{1,0:T(8,128)(2,1)S(1)}, bf16[496,128]{1,0:T(8,128)(2,1)S(1)}, u32[]{:S(2)}, u32[]{:S(2)}) %collective-permute-start.32) | collective-permute-done | bytes 127008 | tf_op jit(solution)/shard_map/ppermute | solution.py:344
  117.4 1.2 %place.1 = (bf16[136,256]{1,0:T(8,128)(2,1)}, bf16[136,256]{1,0:T(8,128)(2,1)}, bf16[136,256]{1,0:T(8,128)(2,1)}, f32[256,32]{1,0:T(8,128)S(1)}) custom-call(s32[5]{0:T(128)S(1)} %stack.23.at_ref, bf16[144,384]{1,0:T(8,128)(2,1)S(1)} %get-tuple-element.104.mine_ref, f32[32,256]{1,0:T(8,128)S(1)} %get-tuple-element.105.wmine_ref, ...), custom_call_target="tpu_custom_call" | custom-call | tf_op jit(solution)/shard_map/place/pallas_call | solution.py:48
  118.6 0.7 copy.11
  (36 shorter events, 0.1 us)
Async XLA Ops:
  0.6 22.4 %collective-permute-start = (bf16[136,512]{1,0:T(8,128)(2,1)}, bf16[136,512]{1,0:T(8,128)(2,1)S(1)}, u32[]{:S(2)}, u32[]{:S(2)}) collective-permute-start(bf16[136,512]{1,0:T(8,128)(2,1)} %dy0_ref.3), channel_id=1, source_target_pairs={{0,1},{1,2},{2,3},{3,0},{4,5},{5,6},{6,7},{7,4},{8,9},{9,10},{10,1... | collective-permute-start | bytes 417800 | tf_op jit(solution)/shard_map/ppermute | solution.py:340
  2.3 23.5 %collective-permute-start.1 = (bf16[136,512]{1,0:T(8,128)(2,1)}, bf16[136,512]{1,0:T(8,128)(2,1)S(1)}, u32[]{:S(2)}, u32[]{:S(2)}) collective-permute-start(bf16[136,512]{1,0:T(8,128)(2,1)} %dy0_ref.3), channel_id=1, source_target_pairs={{0,2},{1,3},{2,0},{3,1},{4,6},{5,7},{6,4},{7,5},{8,10},{9,11},{10,... | collective-permute-start | bytes 417800 | tf_op jit(solution)/shard_map/ppermute | solution.py:340
  5.0 20.8 %collective-permute-start.2 = (bf16[136,512]{1,0:T(8,128)(2,1)}, bf16[136,512]{1,0:T(8,128)(2,1)S(1)}, u32[]{:S(2)}, u32[]{:S(2)}) collective-permute-start(bf16[136,512]{1,0:T(8,128)(2,1)} %dy0_ref.3), channel_id=1, source_target_pairs={{0,3},{1,0},{2,1},{3,2},{4,7},{5,4},{6,5},{7,6},{8,11},{9,8},{10,9... | collective-permute-start | bytes 417800 | tf_op jit(solution)/shard_map/ppermute | solution.py:340
  6.4 0.9 copy-start.4
  7.3 0.9 copy-start.5
  8.2 0.9 copy-start.6
  10.0 4.4 %collective-permute-start.7 = (bf16[144,256]{1,0:T(8,128)(2,1)S(1)}, bf16[144,256]{1,0:T(8,128)(2,1)S(1)}, u32[]{:S(2)}, u32[]{:S(2)}) collective-permute-start(bf16[144,256]{1,0:T(8,128)(2,1)S(1)} %get-tuple-element.63), channel_id=1, source_target_pairs={{0,32},{32,0},{1,33},{33,1},{2,34},{34,2},{3,35},{35,3},{4,36},{36... | collective-permute-start | bytes 221192 | tf_op jit(solution)/shard_map/ppermute | solution.py:344
  14.4 23.3 %collective-permute-start.8 = (bf16[288,256]{1,0:T(8,128)(2,1)S(1)}, bf16[288,256]{1,0:T(8,128)(2,1)S(1)}, u32[]{:S(2)}, u32[]{:S(2)}) collective-permute-start(bf16[288,256]{1,0:T(8,128)(2,1)S(1)} %constant_dynamic-update-slice_fusion.2.refs_4_), channel_id=1, source_target_pairs={{0,64},{64,128},{128,192},{192,0},{1,65},{65,129},{129,193},{193,1... | collective-permute-start | bytes 442376 | tf_op jit(solution)/shard_map/ppermute | solution.py:340
  17.7 22.8 %collective-permute-start.9 = (bf16[288,256]{1,0:T(8,128)(2,1)S(1)}, bf16[288,256]{1,0:T(8,128)(2,1)S(1)}, u32[]{:S(2)}, u32[]{:S(2)}) collective-permute-start(bf16[288,256]{1,0:T(8,128)(2,1)S(1)} %constant_dynamic-update-slice_fusion.2.refs_4_), channel_id=1, source_target_pairs={{0,128},{64,192},{128,0},{192,64},{1,129},{65,193},{129,1},{193,65... | collective-permute-start | bytes 442376 | tf_op jit(solution)/shard_map/ppermute | solution.py:340
  23.1 18.9 %collective-permute-start.10 = (bf16[288,256]{1,0:T(8,128)(2,1)S(1)}, bf16[288,256]{1,0:T(8,128)(2,1)S(1)}, u32[]{:S(2)}, u32[]{:S(2)}) collective-permute-start(bf16[288,256]{1,0:T(8,128)(2,1)S(1)} %constant_dynamic-update-slice_fusion.2.refs_4_), channel_id=1, source_target_pairs={{0,192},{64,0},{128,64},{192,128},{1,193},{65,1},{129,65},{193,129... | collective-permute-start | bytes 442376 | tf_op jit(solution)/shard_map/ppermute | solution.py:340
  25.7 16.2 %collective-permute-start.11 = (bf16[288,256]{1,0:T(8,128)(2,1)S(1)}, bf16[288,256]{1,0:T(8,128)(2,1)S(1)}, u32[]{:S(2)}, u32[]{:S(2)}) collective-permute-start(bf16[288,256]{1,0:T(8,128)(2,1)S(1)} %constant_dynamic-update-slice_fusion.2.refs_4_), channel_id=1, source_target_pairs={{0,4},{4,0},{1,5},{5,1},{2,6},{6,2},{3,7},{7,3},{8,12},{12,8},{9,1... | collective-permute-start | bytes 442376 | tf_op jit(solution)/shard_map/ppermute | solution.py:344
  25.7 1.2 %copy-start = (bf16[256,2048]{1,0:T(8,128)(2,1)S(1)}, bf16[256,2048]{1,0:T(8,128)(2,1)}, u32[]{:S(2)}) copy-start(bf16[256,2048]{1,0:T(8,128)(2,1)} %wo_ref.3) | copy-start | bytes 3145732
  27.0 0.9 copy-start.2
  28.9 7.3 %collective-permute-start.3 = (bf16[144,256]{1,0:T(8,128)(2,1)S(1)}, bf16[144,256]{1,0:T(8,128)(2,1)S(1)}, u32[]{:S(2)}, u32[]{:S(2)}) collective-permute-start(bf16[144,256]{1,0:T(8,128)(2,1)S(1)} %get-tuple-element.61), channel_id=1, source_target_pairs={{0,32},{32,0},{1,33},{33,1},{2,34},{34,2},{3,35},{35,3},{4,36},{36... | collective-permute-start | bytes 221192 | tf_op jit(solution)/shard_map/ppermute | solution.py:344
  36.3 7.9 %collective-permute-start.4 = (bf16[288,256]{1,0:T(8,128)(2,1)S(1)}, bf16[288,256]{1,0:T(8,128)(2,1)S(1)}, u32[]{:S(2)}, u32[]{:S(2)}) collective-permute-start(bf16[288,256]{1,0:T(8,128)(2,1)S(1)} %constant_dynamic-update-slice_fusion.refs_0_), channel_id=1, source_target_pairs={{0,8},{8,16},{16,24},{24,0},{1,9},{9,17},{17,25},{25,1},{2,10},{10... | collective-permute-start | bytes 442376 | tf_op jit(solution)/shard_map/ppermute | solution.py:340
  37.7 8.2 %collective-permute-start.5 = (bf16[288,256]{1,0:T(8,128)(2,1)S(1)}, bf16[288,256]{1,0:T(8,128)(2,1)S(1)}, u32[]{:S(2)}, u32[]{:S(2)}) collective-permute-start(bf16[288,256]{1,0:T(8,128)(2,1)S(1)} %constant_dynamic-update-slice_fusion.refs_0_), channel_id=1, source_target_pairs={{0,16},{8,24},{16,0},{24,8},{1,17},{9,25},{17,1},{25,9},{2,18},{10... | collective-permute-start | bytes 442376 | tf_op jit(solution)/shard_map/ppermute | solution.py:340
  40.5 5.5 %collective-permute-start.6 = (bf16[288,256]{1,0:T(8,128)(2,1)S(1)}, bf16[288,256]{1,0:T(8,128)(2,1)S(1)}, u32[]{:S(2)}, u32[]{:S(2)}) collective-permute-start(bf16[288,256]{1,0:T(8,128)(2,1)S(1)} %constant_dynamic-update-slice_fusion.refs_0_), channel_id=1, source_target_pairs={{0,24},{8,0},{16,8},{24,16},{1,25},{9,1},{17,9},{25,17},{2,26},{10... | collective-permute-start | bytes 442376 | tf_op jit(solution)/shard_map/ppermute | solution.py:340
  41.9 4.1 %collective-permute-start.12 = (bf16[288,256]{1,0:T(8,128)(2,1)S(1)}, bf16[288,256]{1,0:T(8,128)(2,1)S(1)}, u32[]{:S(2)}, u32[]{:S(2)}) collective-permute-start(bf16[288,256]{1,0:T(8,128)(2,1)S(1)} %collective-permute-done.8.refs_5_), channel_id=1, source_target_pairs={{0,4},{4,0},{1,5},{5,1},{2,6},{6,2},{3,7},{7,3},{8,12},{12,8},{9,1... | collective-permute-start | bytes 442376 | tf_op jit(solution)/shard_map/ppermute | solution.py:344
  41.9 4.1 %collective-permute-start.13 = (bf16[288,256]{1,0:T(8,128)(2,1)S(1)}, bf16[288,256]{1,0:T(8,128)(2,1)S(1)}, u32[]{:S(2)}, u32[]{:S(2)}) collective-permute-start(bf16[288,256]{1,0:T(8,128)(2,1)S(1)} %collective-permute-done.9.refs_6_), channel_id=1, source_target_pairs={{0,4},{4,0},{1,5},{5,1},{2,6},{6,2},{3,7},{7,3},{8,12},{12,8},{9,1... | collective-permute-start | bytes 442376 | tf_op jit(solution)/shard_map/ppermute | solution.py:344
  44.2 1.8 %collective-permute-start.14 = (bf16[288,256]{1,0:T(8,128)(2,1)S(1)}, bf16[288,256]{1,0:T(8,128)(2,1)S(1)}, u32[]{:S(2)}, u32[]{:S(2)}) collective-permute-start(bf16[288,256]{1,0:T(8,128)(2,1)S(1)} %collective-permute-done.10.refs_7_), channel_id=1, source_target_pairs={{0,4},{4,0},{1,5},{5,1},{2,6},{6,2},{3,7},{7,3},{8,12},{12,8},{9,1... | collective-permute-start | bytes 442376 | tf_op jit(solution)/shard_map/ppermute | solution.py:344
  51.0 5.4 %collective-permute-start.15 = (bf16[368,128]{1,0:T(8,128)(2,1)S(1)}, bf16[368,128]{1,0:T(8,128)(2,1)S(1)}, u32[]{:S(2)}, u32[]{:S(2)}) collective-permute-start(bf16[368,128]{1,0:T(8,128)(2,1)S(1)} %get-tuple-element.65), channel_id=1, source_target_pairs={{0,24},{8,0},{16,8},{24,16},{1,25},{9,1},{17,9},{25,17},{2,26},{10... | collective-permute-start | bytes 282632 | tf_op jit(solution)/shard_map/ppermute | solution.py:340
  53.7 6.1 %collective-permute-start.16 = (bf16[368,128]{1,0:T(8,128)(2,1)S(1)}, bf16[368,128]{1,0:T(8,128)(2,1)S(1)}, u32[]{:S(2)}, u32[]{:S(2)}) collective-permute-start(bf16[368,128]{1,0:T(8,128)(2,1)S(1)} %get-tuple-element.66), channel_id=1, source_target_pairs={{0,16},{8,24},{16,0},{24,8},{1,17},{9,25},{17,1},{25,9},{2,18},{10... | collective-permute-start | bytes 282632 | tf_op jit(solution)/shard_map/ppermute | solution.py:340
  54.5 6.2 %collective-permute-start.17 = (bf16[368,128]{1,0:T(8,128)(2,1)S(1)}, bf16[368,128]{1,0:T(8,128)(2,1)S(1)}, u32[]{:S(2)}, u32[]{:S(2)}) collective-permute-start(bf16[368,128]{1,0:T(8,128)(2,1)S(1)} %get-tuple-element.67), channel_id=1, source_target_pairs={{0,8},{8,16},{16,24},{24,0},{1,9},{9,17},{17,25},{25,1},{2,10},{10... | collective-permute-start | bytes 282632 | tf_op jit(solution)/shard_map/ppermute | solution.py:340
  60.8 9.3 %copy-start.1 = (bf16[256,2048]{1,0:T(8,128)(2,1)S(1)}, bf16[256,2048]{1,0:T(8,128)(2,1)}, u32[]{:S(2)}) copy-start(bf16[256,2048]{1,0:T(8,128)(2,1)} %wo_ref.3) | copy-start | bytes 3145732
  60.8 9.3 %copy-start.3 = (bf16[136,512]{1,0:T(8,128)(2,1)S(1)}, bf16[136,512]{1,0:T(8,128)(2,1)}, u32[]{:S(2)}) copy-start(bf16[136,512]{1,0:T(8,128)(2,1)} %dy0_ref.3) | copy-start | bytes 417796
  64.9 10.7 %collective-permute-start.22 = (bf16[4,288,256]{2,1,0:T(8,128)(2,1)S(1)}, bf16[4,288,256]{2,1,0:T(8,128)(2,1)S(1)}, u32[]{:S(2)}, u32[]{:S(2)}) collective-permute-start(bf16[4,288,256]{2,1,0:T(8,128)(2,1)S(1)} %get-tuple-element.84), channel_id=1, source_target_pairs={{0,4},{4,0},{1,5},{5,1},{2,6},{6,2},{3,7},{7,3},{8,12},{12,8},{9,1... | collective-permute-start | bytes 1769480 | tf_op jit(solution)/shard_map/ppermute | solution.py:344
  65.8 4.3 %collective-permute-start.18 = (bf16[144,128]{1,0:T(8,128)(2,1)S(1)}, bf16[144,128]{1,0:T(8,128)(2,1)S(1)}, u32[]{:S(2)}, u32[]{:S(2)}) collective-permute-start(bf16[144,128]{1,0:T(8,128)(2,1)S(1)} %get-tuple-element.69), channel_id=1, source_target_pairs={{0,32},{32,0},{1,33},{33,1},{2,34},{34,2},{3,35},{35,3},{4,36},{36... | collective-permute-start | bytes 110600 | tf_op jit(solution)/shard_map/ppermute | solution.py:344
  71.4 4.2 %collective-permute-start.23 = (bf16[4,256,256]{2,1,0:T(8,128)(2,1)S(1)}, bf16[4,256,256]{2,1,0:T(8,128)(2,1)S(1)}, u32[]{:S(2)}, u32[]{:S(2)}) collective-permute-start(bf16[4,256,256]{2,1,0:T(8,128)(2,1)S(1)} %get-tuple-element.86), channel_id=1, source_target_pairs={{0,4},{4,0},{1,5},{5,1},{2,6},{6,2},{3,7},{7,3},{8,12},{12,8},{9,1... | collective-permute-start | bytes 1572872 | tf_op jit(solution)/shard_map/ppermute | solution.py:344
  75.9 7.9 %collective-permute-start.27 = (bf16[800,128]{1,0:T(8,128)(2,1)S(1)}, bf16[800,128]{1,0:T(8,128)(2,1)S(1)}, u32[]{:S(2)}, u32[]{:S(2)}) collective-permute-start(bf16[800,128]{1,0:T(8,128)(2,1)S(1)} %get-tuple-element.96), channel_id=1, source_target_pairs={{0,24},{8,0},{16,8},{24,16},{1,25},{9,1},{17,9},{25,17},{2,26},{10... | collective-permute-start | bytes 614408 | tf_op jit(solution)/shard_map/ppermute | solution.py:340
  76.5 9.5 %collective-permute-start.28 = (bf16[800,128]{1,0:T(8,128)(2,1)S(1)}, bf16[800,128]{1,0:T(8,128)(2,1)S(1)}, u32[]{:S(2)}, u32[]{:S(2)}) collective-permute-start(bf16[800,128]{1,0:T(8,128)(2,1)S(1)} %get-tuple-element.97), channel_id=1, source_target_pairs={{0,16},{8,24},{16,0},{24,8},{1,17},{9,25},{17,1},{25,9},{2,18},{10... | collective-permute-start | bytes 614408 | tf_op jit(solution)/shard_map/ppermute | solution.py:340
  77.4 12.2 %collective-permute-start.29 = (bf16[800,128]{1,0:T(8,128)(2,1)S(1)}, bf16[800,128]{1,0:T(8,128)(2,1)S(1)}, u32[]{:S(2)}, u32[]{:S(2)}) collective-permute-start(bf16[800,128]{1,0:T(8,128)(2,1)S(1)} %get-tuple-element.98), channel_id=1, source_target_pairs={{0,8},{8,16},{16,24},{24,0},{1,9},{9,17},{17,25},{25,1},{2,10},{10... | collective-permute-start | bytes 614408 | tf_op jit(solution)/shard_map/ppermute | solution.py:340
  78.4 19.2 %collective-permute-start.24 = (bf16[288,256]{1,0:T(8,128)(2,1)S(1)}, bf16[288,256]{1,0:T(8,128)(2,1)S(1)}, u32[]{:S(2)}, u32[]{:S(2)}) collective-permute-start(bf16[288,256]{1,0:T(8,128)(2,1)S(1)} %get-tuple-element.91), channel_id=1, source_target_pairs={{0,192},{64,0},{128,64},{192,128},{1,193},{65,1},{129,65},{193,129... | collective-permute-start | bytes 442376 | tf_op jit(solution)/shard_map/ppermute | solution.py:340
  89.7 10.8 %collective-permute-start.30 = (bf16[128,256]{1,0:T(8,128)(2,1)S(1)}, bf16[128,256]{1,0:T(8,128)(2,1)S(1)}, u32[]{:S(2)}, u32[]{:S(2)}) collective-permute-start(bf16[128,256]{1,0:T(8,128)(2,1)S(1)} %get-tuple-element.101), channel_id=1, source_target_pairs={{0,192},{64,128},{128,64},{192,0},{1,193},{65,129},{129,65},{193,1... | collective-permute-start | bytes 196616 | tf_op jit(solution)/shard_map/ppermute | solution.py:344
  92.5 14.9 %collective-permute-start.25 = (bf16[288,256]{1,0:T(8,128)(2,1)S(1)}, bf16[288,256]{1,0:T(8,128)(2,1)S(1)}, u32[]{:S(2)}, u32[]{:S(2)}) collective-permute-start(bf16[288,256]{1,0:T(8,128)(2,1)S(1)} %get-tuple-element.92), channel_id=1, source_target_pairs={{0,128},{64,192},{128,0},{192,64},{1,129},{65,193},{129,1},{193,65... | collective-permute-start | bytes 442376 | tf_op jit(solution)/shard_map/ppermute | solution.py:340
  93.7 13.8 %collective-permute-start.26 = (bf16[288,256]{1,0:T(8,128)(2,1)S(1)}, bf16[288,256]{1,0:T(8,128)(2,1)S(1)}, u32[]{:S(2)}, u32[]{:S(2)}) collective-permute-start(bf16[288,256]{1,0:T(8,128)(2,1)S(1)} %get-tuple-element.93), channel_id=1, source_target_pairs={{0,64},{64,128},{128,192},{192,0},{1,65},{65,129},{129,193},{193,1... | collective-permute-start | bytes 442376 | tf_op jit(solution)/shard_map/ppermute | solution.py:340
  96.3 16.2 %collective-permute-start.21 = (bf16[136,512]{1,0:T(8,128)(2,1)S(1)}, bf16[136,512]{1,0:T(8,128)(2,1)S(1)}, u32[]{:S(2)}, u32[]{:S(2)}) collective-permute-start(bf16[136,512]{1,0:T(8,128)(2,1)S(1)} %get-tuple-element.79), channel_id=1, source_target_pairs={{0,3},{1,0},{2,1},{3,2},{4,7},{5,4},{6,5},{7,6},{8,11},{9,8},{10,9... | collective-permute-start | bytes 417800 | tf_op jit(solution)/shard_map/ppermute | solution.py:340
  97.6 14.8 %collective-permute-start.20 = (bf16[136,512]{1,0:T(8,128)(2,1)S(1)}, bf16[136,512]{1,0:T(8,128)(2,1)S(1)}, u32[]{:S(2)}, u32[]{:S(2)}) collective-permute-start(bf16[136,512]{1,0:T(8,128)(2,1)S(1)} %get-tuple-element.78), channel_id=1, source_target_pairs={{0,2},{1,3},{2,0},{3,1},{4,6},{5,7},{6,4},{7,5},{8,10},{9,11},{10,... | collective-permute-start | bytes 417800 | tf_op jit(solution)/shard_map/ppermute | solution.py:340
  100.5 12.0 %collective-permute-start.19 = (bf16[136,512]{1,0:T(8,128)(2,1)S(1)}, bf16[136,512]{1,0:T(8,128)(2,1)S(1)}, u32[]{:S(2)}, u32[]{:S(2)}) collective-permute-start(bf16[136,512]{1,0:T(8,128)(2,1)S(1)} %get-tuple-element.77), channel_id=1, source_target_pairs={{0,1},{1,2},{2,3},{3,0},{4,5},{5,6},{6,7},{7,4},{8,9},{9,10},{10,1... | collective-permute-start | bytes 417800 | tf_op jit(solution)/shard_map/ppermute | solution.py:340
  107.3 4.9 %collective-permute-start.31 = (bf16[64,256]{1,0:T(8,128)(2,1)S(1)}, bf16[64,256]{1,0:T(8,128)(2,1)S(1)}, u32[]{:S(2)}, u32[]{:S(2)}) collective-permute-start(bf16[64,256]{1,0:T(8,128)(2,1)S(1)} %get-tuple-element.103), channel_id=1, source_target_pairs={{0,64},{64,0},{128,192},{192,128},{1,65},{65,1},{129,193},{193,129... | collective-permute-start | bytes 98312 | tf_op jit(solution)/shard_map/ppermute | solution.py:344
  112.3 5.0 %collective-permute-start.32 = (bf16[496,128]{1,0:T(8,128)(2,1)S(1)}, bf16[496,128]{1,0:T(8,128)(2,1)S(1)}, u32[]{:S(2)}, u32[]{:S(2)}) collective-permute-start(bf16[496,128]{1,0:T(8,128)(2,1)S(1)} %get-tuple-element.106), channel_id=1, source_target_pairs={{0,32},{32,0},{1,33},{33,1},{2,34},{34,2},{3,35},{35,3},{4,36},{36... | collective-permute-start | bytes 380936 | tf_op jit(solution)/shard_map/ppermute | solution.py:344
where the time goes:
time: 120 us; the launch traced here: 119 us
  waiting for transfers between devices  47.6 us (40%)
  starting transfers between devices  44.8 us (37%)
  Pallas kernels  19 us (16%)
  local copies, waits for them, and re-layouts  5.58 us (5%)
  other arithmetic  1.42 us (1%)
    ppermute x21, starting transfers between devices, shifted(): lax.ppermute(value, axis, [(i, (i + by) % size) for i in range(size)])  37 us
    ppermute x21, waiting for transfers between devices, shifted(): lax.ppermute(value, axis, [(i, (i + by) % size) for i in range(size)])  24.1 us
    ppermute x12, waiting for transfers between devices, swapped(): return lax.ppermute(value, axis, [(i, i ^ mask) for i in range(size)])  23.5 us
    pallas_call x12, Pallas kernels, call(): pl.pallas_call(kernel, in_specs=[SMEM] * scalars + [pl.BlockSpec(memory_s...  19 us
    ppermute x12, starting transfers between devices, swapped(): return lax.ppermute(value, axis, [(i, i ^ mask) for i in range(size)])  7.86 us
    unnamed x17, local copies, waits for them, and re-layouts  5.48 us
  transfers between devices with their start and end apart: 33, of which 16 were waited for; matrix products, arithmetic and copies ran while one was open for 1% of the time, Pallas kernels for 7%

commit v1 on v0

--- a/solution.py
+++ b/solution.py
@@ -42,12 +42,11 @@
     return jax.ShapeDtypeStruct(dims, kind)
 
 
-def call(kernel, name, ins, outs, scratch=(), scalars=0, far=0, flops=0):
-    near = len(ins) - scalars - far
+def call(kernel, name, ins, outs, scratch=(), scalars=0, flops=0):
     cost = pl.CostEstimate(flops=flops, bytes_accessed=1 << 20, transcendentals=0) if flops else None
     return pl.pallas_call(
         kernel,
-        in_specs=[SMEM] * scalars + [pl.BlockSpec(memory_space=pl.ANY)] * far + [VMEM] * near,
+        in_specs=[SMEM] * scalars + [VMEM] * (len(ins) - scalars),
         out_shape=outs,
         scratch_shapes=list(scratch),
         compiler_params=PARAMS,
@@ -68,37 +67,26 @@
         send_ref[...] = first
 
 
-def pack_kernel(at_ref, q_hbm, k_hbm, v_hbm, ids_ref, keep_ref, send_ref, qkeep_ref, qsend_ref, here_ref, sems):
-    copies = [
-        pltpu.make_async_copy(ref, here_ref.at[i], sems.at[i]) for i, ref in enumerate((q_hbm, k_hbm, v_hbm))
-    ]
-    for copy in copies:
-        copy.start()
+def pack_kernel(at_ref, qkv_ref, ids_ref, keep_ref, send_ref, qkeep_ref, qsend_ref):
     ids = ids_ref[...].astype(BF16)
     zero = jnp.zeros((8, DH), BF16)
-    for copy in copies:
-        copy.wait()
     kvs, qs = [], []
     for head in range(2):
         cols = slice(head * DH, (head + 1) * DH)
-        k = jnp.concatenate([here_ref[1, :, cols], ids], axis=0)
-        v = jnp.concatenate([here_ref[2, :, cols], zero], axis=0)
+        k = jnp.concatenate([qkv_ref[1, :, cols], ids], axis=0)
+        v = jnp.concatenate([qkv_ref[2, :, cols], zero], axis=0)
         kvs.append(jnp.concatenate([k, v], axis=1))
-        qs.append(jnp.concatenate([here_ref[0, :, cols], ids], axis=0))
+        qs.append(jnp.concatenate([qkv_ref[0, :, cols], ids], axis=0))
     by_parity(at_ref[0], kvs[0], kvs[1], keep_ref, send_ref)
     by_parity(at_ref[0], qs[0], qs[1], qkeep_ref, qsend_ref)
 
 
-def dattn_kernel(at_ref, dy0_ref, dy1_ref, dy2_ref, dy3_ref, wo_ref, ids_ref, qkeep_ref, qsend_ref, keep_ref, send_ref):
-    h = at_ref[1]
+def dattn_kernel(at_ref, dy0_ref, dy1_ref, dy2_ref, dy3_ref, wo_ref, qkeep_ref, qsend_ref, keep_ref, send_ref):
     acc = jnp.zeros((ROWS, FEATS), F32)
     for s, ref in enumerate((dy0_ref, dy1_ref, dy2_ref, dy3_ref)):
-        start = pl.multiple_of(lax.rem(h - s + NH, NH) * WIDE, WIDE)
-        acc = acc + lax.dot_general(ref[...], wo_ref[:, pl.ds(start, WIDE)], LAST, preferred_element_type=F32)
-    ids = ids_ref[...].T
-    real = jnp.concatenate([ids[:, 0:1], ids[0:8, 1:2]], axis=0) >= 0.0
-    acc = jnp.where(real, acc, 0.0).astype(BF16)
-    acc = jnp.concatenate([acc, jnp.zeros((PAD - ROWS, FEATS), BF16)], axis=0)
+        block = wo_ref[:, s * WIDE : (s + 1) * WIDE]
+        acc = acc + lax.dot_general(ref[...], block, LAST, preferred_element_type=F32)
+    acc = jnp.concatenate([acc.astype(BF16), jnp.zeros((PAD - ROWS, FEATS), BF16)], axis=0)
     keep_ref[:, 0:DH] = qkeep_ref[...]
     send_ref[:, 0:DH] = qsend_ref[...]
     by_parity(at_ref[0], acc[:, 0:DH], acc[:, DH:FEATS], keep_ref.at[:, DH:FEATS], send_ref.at[:, DH:FEATS])
@@ -263,8 +251,8 @@
     even = e == 0
     attn = jnp.concatenate([jnp.where(even, mine, other), jnp.where(even, other, mine)], axis=1)
     for s in range(NH):
-        start = pl.multiple_of(lax.rem(h + s, NH) * WIDE, WIDE)
-        part = jnp.dot(attn, wo_ref[:, pl.ds(start, WIDE)], preferred_element_type=F32)
+        at = -s % NH * WIDE
+        part = jnp.dot(attn, wo_ref[:, at : at + WIDE], preferred_element_type=F32)
         out_refs[s][...] = part[0:ROWS].astype(BF16)
     for s, ref in enumerate((dy0_ref, dy1_ref, dy2_ref, dy3_ref)):
         dwo_ref[s] = lax.dot_general(ref[...], attn[0:ROWS], FIRST, preferred_element_type=F32).astype(BF16)
@@ -333,7 +321,7 @@
         ref[:, 0:DH] = jnp.where(even, mine, other)
         ref[:, DH:FEATS] = jnp.where(even, other, mine)
     got = got_ref[3 * PAD : 3 * PAD + 2 * COLS].astype(F32)
-    dwo_ref[...] = (wmine_ref[...] + jnp.concatenate([got[0:COLS], got[COLS : 2 * COLS]], axis=1)).T
+    dwo_ref[...] = wmine_ref[...] + jnp.concatenate([got[0:COLS], got[COLS : 2 * COLS]], axis=1)
 
 
 def shifted(value, axis, size, by):
@@ -357,17 +345,23 @@
     keep, send, qkeep, qsend = call(
         pack_kernel,
         "pack",
-        [at, queries, key_rows, value_rows, ids],
+        [at, jnp.stack([queries, key_rows, value_rows]), ids],
         [shape((PAD, FEATS))] * 2 + [shape((PAD, DH))] * 2,
-        [pltpu.VMEM((3, ROWS, FEATS), BF16), pltpu.SemaphoreType.DMA((3,))],
         scalars=1,
-        far=3,
-    )
-    kvs = around(jnp.concatenate([keep, swapped(send, "e", 2, 1)], axis=0), "zr")
-    dys = around(dy, "head")
+    )
+    kv = jnp.concatenate([keep, swapped(send, "e", 2, 1)], axis=0)
+    dy, send = lax.optimization_barrier((dy, send))
+    dys = around(jnp.where(scale_of[:, None] >= 0, dy, 0), "head")
+    wo, _ = lax.optimization_barrier((wo, dys[0]))
+    at_head = lax.axis_index("head")
+    wo = jnp.concatenate(
+        [lax.dynamic_slice_in_dim(wo, lax.rem(at_head - s + NH, NH) * WIDE, WIDE, 1) for s in range(NH)], axis=1
+    )
     keep, send = call(
-        dattn_kernel, "dattn", [at, *dys, wo, ids, qkeep, qsend], [shape((PAD, FEATS))] * 2, scalars=1
-    )
+        dattn_kernel, "dattn", [at, *dys, wo, qkeep, qsend], [shape((PAD, FEATS))] * 2, scalars=1
+    )
+    kv_late, send = lax.optimization_barrier((kv, send))
+    kvs = [kv, shifted(kv, "zr", 4, 1), shifted(kv_late, "zr", 4, 2), shifted(kv, "zr", 4, 3)]
     qs = around(jnp.concatenate([keep, swapped(send, "e", 2, 1)], axis=0), "x")
     kvs = kvs + [swapped(one, "c", 2, 1) for one in kvs]
 
@@ -383,6 +377,7 @@
 
     keep, send = call(merge_kernel, "merge", loads, [shape((PAD, DH))] * 2)
     other = swapped(send, "e", 2, 1)
+    q, send = lax.optimization_barrier((q, send))
     scratch = [pltpu.VMEM((NQ, FEATS), BF16), pltpu.VMEM((NQ, NQ), BF16)]
     dkv_send, dq_part = call(
         functools.partial(backward_kernel, NQ),
@@ -418,6 +413,7 @@
     )
     dkvs = [mine] + [shifted(far[s - 1], "zr", 4, -s) for s in (1, 2, 3)]
     xs = [shifted(far[3 + s], "x", 4, -s) for s in (1, 2, 3)]
+    xs, dkvs = lax.optimization_barrier((xs, dkvs))
     dq, wkeep, wsend = call(
         ring_kernel,
         "ring",
@@ -443,10 +439,10 @@
         place_kernel,
         "place",
         [at, keep, wkeep, swapped(send, "e", 2, 1)],
-        [shape((ROWS, FEATS))] * 3 + [shape((FEATS, COLS), F32)],
+        [shape((ROWS, FEATS))] * 3 + [shape((COLS, FEATS), F32)],
         scalars=1,
     )
-    return (block_out, dq, dk, dv, dwo)
+    return (block_out, dq, dk, dv, dwo.T)
 
 
 def solution(mesh):

time: 120 us -> 115 us (0.958)
  local copies, waits for them, and re-layouts: 5.58 us -> 0.22 us
  waiting for transfers between devices: 47.6 us -> 42.9 us
  other arithmetic: 1.42 us -> 4.28 us
  starting transfers between devices: 44.8 us -> 47.2 us
    ppermute x12, waiting for transfers between devices: 23.5 us -> 17.7 us  [swapped(): return lax.ppermute(value, axis, [(i, i ^ mask) for i in range(size)])]
    unnamed x17 -> x4, local copies, waits for them, and re-layouts: 5.48 us -> 0.02 us
    ppermute x12, starting transfers between devices: 7.86 us -> 9.51 us  [swapped(): return lax.ppermute(value, axis, [(i, i ^ mask) for i in range(size)])]
  transfers between devices with their start and end apart: 33 -> 33, of which waited for: 16 -> 14; matrix products, arithmetic and copies ran while one was open for 1% -> 2% of each run, Pallas kernels for 7% -> 6%
where the time goes in v1:
time: 115 us; the launch traced here: 114 us
  starting transfers between devices  47.2 us (41%)
  waiting for transfers between devices  42.9 us (37%)
  Pallas kernels  18.5 us (16%)
  other arithmetic  4.28 us (4%)
    ppermute x21, starting transfers between devices, shifted(): lax.ppermute(value, axis, [(i, (i + by) % size) for i in range(size)])  37.7 us
    ppermute x21, waiting for transfers between devices, shifted(): lax.ppermute(value, axis, [(i, (i + by) % size) for i in range(size)])  25.2 us
    pallas_call x12, Pallas kernels, call(): pl.pallas_call(kernel, in_specs=[SMEM] * scalars + [VMEM] * (len(ins) - s...  18.5 us
    ppermute x12, waiting for transfers between devices, swapped(): return lax.ppermute(value, axis, [(i, i ^ mask) for i in range(size)])  17.7 us
    ppermute x12, starting transfers between devices, swapped(): return lax.ppermute(value, axis, [(i, i ^ mask) for i in range(size)])  9.51 us
  transfers between devices with their start and end apart: 33, of which 14 were waited for; matrix products, arithmetic and copies ran while one was open for 2% of the time, Pallas kernels for 6%

profile of v1, /device:TPU:8, one launch (start us, length us, event | category | flops | bytes accessed | tf_op | source)
XLA Modules:
  0.0 114.0 jit_solution(6326328992640195703)
XLA Ops:
  0.6 0.8 convert_bitcast_fusion.ids_ref
  1.4 1.0 pad_maximum_fusion.1.qkv_ref
  2.4 0.1 stack.35.at_ref
  2.5 0.6 pack.1
  3.1 2.0 %collective-permute-start.3 = (bf16[144,256]{1,0:T(8,128)(2,1)S(1)}, bf16[144,256]{1,0:T(8,128)(2,1)S(1)}, u32[]{:S(2)}, u32[]{:S(2)}) collective-permute-start(bf16[144,256]{1,0:T(8,128)(2,1)S(1)} %get-tuple-element.70), channel_id=1, source_target_pairs={{0,32},{32,0},{1,33},{33,1},{2,34},{34,2},{3,35},{35,3},{4,36},{36... | collective-permute-start | bytes 221192 | tf_op jit(solution)/shard_map/ppermute | solution.py:332
  5.1 0.7 broadcast_compare_fusion
  5.8 1.0 broadcast_select_fusion.dy0_ref
  6.8 0.5 collective-permute-start.2
  7.3 2.6 %collective-permute-start.1 = (bf16[136,512]{1,0:T(8,128)(2,1)S(1)}, bf16[136,512]{1,0:T(8,128)(2,1)S(1)}, u32[]{:S(2)}, u32[]{:S(2)}) collective-permute-start(bf16[136,512]{1,0:T(8,128)(2,1)S(1)} %broadcast_select_fusion.dy0_ref), channel_id=1, source_target_pairs={{0,2},{1,3},{2,0},{3,1},{4,6},{5,7},{6,4},{7,5},{8,10},{9,11},{10,... | collective-permute-start | bytes 417800 | tf_op jit(solution)/shard_map/ppermute | solution.py:328
  9.9 1.9 %collective-permute-start = (bf16[136,512]{1,0:T(8,128)(2,1)S(1)}, bf16[136,512]{1,0:T(8,128)(2,1)S(1)}, u32[]{:S(2)}, u32[]{:S(2)}) collective-permute-start(bf16[136,512]{1,0:T(8,128)(2,1)S(1)} %broadcast_select_fusion.dy0_ref), channel_id=1, source_target_pairs={{0,1},{1,2},{2,3},{3,0},{4,5},{5,6},{6,7},{7,4},{8,9},{9,10},{10,1... | collective-permute-start | bytes 417800 | tf_op jit(solution)/shard_map/ppermute | solution.py:328
  11.8 0.1 constant_dynamic-slice_fusion.3
  11.9 0.1 pad_maximum_fusion.wo_ref
  12.0 0.0 collective-permute-done.3
  12.1 0.1 collective-permute-start.11
  12.2 5.5 %collective-permute-start.10 = (bf16[288,256]{1,0:T(8,128)(2,1)S(1)}, bf16[288,256]{1,0:T(8,128)(2,1)S(1)}, u32[]{:S(2)}, u32[]{:S(2)}) collective-permute-start(bf16[288,256]{1,0:T(8,128)(2,1)S(1)} %constant_dynamic-update-slice_fusion.refs_4_), channel_id=1, source_target_pairs={{0,192},{64,0},{128,64},{192,128},{1,193},{65,1},{129,65},{193,129... | collective-permute-start | bytes 442376 | tf_op jit(solution)/shard_map/ppermute | solution.py:328
  17.7 0.0 collective-permute-done.dy1_ref
  17.7 1.0 dattn.1
  18.7 1.1 collective-permute-start.4
  19.8 5.4 %collective-permute-start.9 = (bf16[288,256]{1,0:T(8,128)(2,1)S(1)}, bf16[288,256]{1,0:T(8,128)(2,1)S(1)}, u32[]{:S(2)}, u32[]{:S(2)}) collective-permute-start(bf16[288,256]{1,0:T(8,128)(2,1)S(1)} %constant_dynamic-update-slice_fusion.refs_4_), channel_id=1, source_target_pairs={{0,128},{64,192},{128,0},{192,64},{1,129},{65,193},{129,1},{193,65... | collective-permute-start | bytes 442376 | tf_op jit(solution)/shard_map/ppermute | solution.py:328
  25.2 3.2 %collective-permute-done.4 = bf16[144,256]{1,0:T(8,128)(2,1)S(1)} collective-permute-done((bf16[144,256]{1,0:T(8,128)(2,1)S(1)}, bf16[144,256]{1,0:T(8,128)(2,1)S(1)}, u32[]{:S(2)}, u32[]{:S(2)}) %collective-permute-start.4) | collective-permute-done | bytes 73760 | tf_op jit(solution)/shard_map/ppermute | solution.py:332
  28.4 2.8 %collective-permute-start.7 = (bf16[288,256]{1,0:T(8,128)(2,1)S(1)}, bf16[288,256]{1,0:T(8,128)(2,1)S(1)}, u32[]{:S(2)}, u32[]{:S(2)}) collective-permute-start(bf16[288,256]{1,0:T(8,128)(2,1)S(1)} %constant_dynamic-update-slice_fusion.2.refs_0_), channel_id=1, source_target_pairs={{0,24},{8,0},{16,8},{24,16},{1,25},{9,1},{17,9},{25,17},{2,26},{10... | collective-permute-start | bytes 442376 | tf_op jit(solution)/shard_map/ppermute | solution.py:328
  31.2 0.8 collective-permute-start.6
  32.0 0.9 collective-permute-start.5
  32.9 1.2 %collective-permute-done.9.refs_6_ = bf16[288,256]{1,0:T(8,128)(2,1)S(1)} collective-permute-done((bf16[288,256]{1,0:T(8,128)(2,1)S(1)}, bf16[288,256]{1,0:T(8,128)(2,1)S(1)}, u32[]{:S(2)}, u32[]{:S(2)}) %collective-permute-start.9) | collective-permute-done | bytes 147488 | tf_op jit(solution)/shard_map/ppermute | solution.py:328
  34.1 3.5 %collective-permute-done.7.refs_3_ = bf16[288,256]{1,0:T(8,128)(2,1)S(1)} collective-permute-done((bf16[288,256]{1,0:T(8,128)(2,1)S(1)}, bf16[288,256]{1,0:T(8,128)(2,1)S(1)}, u32[]{:S(2)}, u32[]{:S(2)}) %collective-permute-start.7) | collective-permute-done | bytes 147488 | tf_op jit(solution)/shard_map/ppermute | solution.py:328
  37.5 0.0 collective-permute-start.13
  37.6 1.9 %collective-permute-done.6.refs_2_ = bf16[288,256]{1,0:T(8,128)(2,1)S(1)} collective-permute-done((bf16[288,256]{1,0:T(8,128)(2,1)S(1)}, bf16[288,256]{1,0:T(8,128)(2,1)S(1)}, u32[]{:S(2)}, u32[]{:S(2)}) %collective-permute-start.6) | collective-permute-done | bytes 147488 | tf_op jit(solution)/shard_map/ppermute | solution.py:328
  39.4 1.8 %collective-permute-done.5.refs_1_ = bf16[288,256]{1,0:T(8,128)(2,1)S(1)} collective-permute-done((bf16[288,256]{1,0:T(8,128)(2,1)S(1)}, bf16[288,256]{1,0:T(8,128)(2,1)S(1)}, u32[]{:S(2)}, u32[]{:S(2)}) %collective-permute-start.5) | collective-permute-done | bytes 147488 | tf_op jit(solution)/shard_map/ppermute | solution.py:328
  41.2 5.0 %forward.1 = (bf16[368,128]{1,0:T(8,128)(2,1)S(1)}, bf16[368,128]{1,0:T(8,128)(2,1)S(1)}, bf16[368,128]{1,0:T(8,128)(2,1)S(1)}, bf16[368,128]{1,0:T(8,128)(2,1)S...) custom-call(bf16[288,256]{1,0:T(8,128)(2,1)S(1)} %constant_dynamic-u, ...), custom_call_target="tpu_custom_call" | custom-call | flops 2038431744 | bytes 1048576 | tf_op jit(solution)/shard_map/forward/pallas_call | solution.py:47
  46.2 1.4 %collective-permute-start.15 = (bf16[368,128]{1,0:T(8,128)(2,1)S(1)}, bf16[368,128]{1,0:T(8,128)(2,1)S(1)}, u32[]{:S(2)}, u32[]{:S(2)}) collective-permute-start(bf16[368,128]{1,0:T(8,128)(2,1)S(1)} %get-tuple-element.81), channel_id=1, source_target_pairs={{0,24},{8,0},{16,8},{24,16},{1,25},{9,1},{17,9},{25,17},{2,26},{10... | collective-permute-start | bytes 282632 | tf_op jit(solution)/shard_map/ppermute | solution.py:328
  47.6 0.0 collective-permute-start.16
  47.7 0.9 collective-permute-start.17
  48.6 3.3 %collective-permute-done.15.l1_ref.refs_1_ = bf16[368,128]{1,0:T(8,128)(2,1)S(1)} collective-permute-done((bf16[368,128]{1,0:T(8,128)(2,1)S(1)}, bf16[368,128]{1,0:T(8,128)(2,1)S(1)}, u32[]{:S(2)}, u32[]{:S(2)}) %collective-permute-start.15) | collective-permute-done | bytes 94240 | tf_op jit(solution)/shard_map/ppermute | solution.py:328
  51.9 2.8 %collective-permute-done.16.l2_ref.refs_2_ = bf16[368,128]{1,0:T(8,128)(2,1)S(1)} collective-permute-done((bf16[368,128]{1,0:T(8,128)(2,1)S(1)}, bf16[368,128]{1,0:T(8,128)(2,1)S(1)}, u32[]{:S(2)}, u32[]{:S(2)}) %collective-permute-start.16) | collective-permute-done | bytes 94240 | tf_op jit(solution)/shard_map/ppermute | solution.py:328
  54.7 0.7 collective-permute-done.17.l3_ref.refs_3_
  55.3 0.8 merge.1
  56.2 4.1 %backward_far.1 = (bf16[4,288,256]{2,1,0:T(8,128)(2,1)S(1)}, f32[1152,128]{1,0:T(8,128)S(1)}) custom-call(bf16[1152,256]{1,0:T(8,128)(2,1)S(1)} %get-tuple-element.87.q_ref, bf16[1152,128]{1,0:T(8,128)(2,1)S(1)} %get-tuple-element.88.qm_ref, bf16[2304,256]{1,0:T(8,128)(2,1)S(1)} %get-tuple-element.89.kv_ref, bf16[2304,128]{1,0:T(8,128)(2,1)S(1)} %get-tuple-element.90.km_ref, ...), custom_call_target="tpu_custom_call" | custom-call | flops 2038431744 | bytes 1048576 | tf_op jit(solution)/shard_map/backward_far/pallas_call | solution.py:47
  60.3 0.1 collective-permute-start.22
  60.4 0.3 collective-permute-start.18
  60.7 3.9 %collective-permute-done.18.other_ref = bf16[144,128]{1,0:T(8,128)(2,1)S(1)} collective-permute-done((bf16[144,128]{1,0:T(8,128)(2,1)S(1)}, bf16[144,128]{1,0:T(8,128)(2,1)S(1)}, u32[]{:S(2)}, u32[]{:S(2)}) %collective-permute-start.18) | collective-permute-done | bytes 36896 | tf_op jit(solution)/shard_map/ppermute | solution.py:332
  64.6 1.2 %project.1 = (bf16[136,512]{1,0:T(8,128)(2,1)S(1)}, bf16[136,512]{1,0:T(8,128)(2,1)S(1)}, bf16[136,512]{1,0:T(8,128)(2,1)S(1)}, bf16[136,512]{1,0:T(8,128)(2,1)S...) custom-call(s32[5]{0:T(128)S(1)} %stack.35.at_ref, ...), custom_call_target="tpu_custom_call" | custom-call | tf_op jit(solution)/shard_map/project/pallas_call | solution.py:47
  65.9 0.1 collective-permute-start.23
  66.0 4.1 %backward_near.1 = (bf16[4,288,256]{2,1,0:T(8,128)(2,1)S(1)}, bf16[288,128]{1,0:T(8,128)(2,1)S(1)}, bf16[288,128]{1,0:T(8,128)(2,1)S(1)}, bf16[288,128]{1,0:T(8,128)(2,1)S(1)}, bf16[288,128]{1,0:T(8,128)(2,1)S(1)}) custom-call(bf16[1152,256]{1,0:T(8,128)(2,1)S(1)} %get-tuple-element.87.q_ref, bf16[1152,128]{1,0:T(8,128)(2,1)S(1)} %get-tuple-element.88.qm_ref, ...), custom_call_target="tpu_custom_call" | custom-call | flops 2038431744 | bytes 1048576 | tf_op jit(solution)/shard_map/backward_near/pallas_call | solution.py:47
  70.1 0.3 core.1
  70.3 1.8 %collective-permute-start.27 = (bf16[288,256]{1,0:T(8,128)(2,1)S(1)}, bf16[288,256]{1,0:T(8,128)(2,1)S(1)}, u32[]{:S(2)}, u32[]{:S(2)}) collective-permute-start(bf16[288,256]{1,0:T(8,128)(2,1)S(1)} %get-tuple-element.111), channel_id=1, source_target_pairs={{0,192},{64,0},{128,64},{192,128},{1,193},{65,1},{129,65},{193,129... | collective-permute-start | bytes 442376 | tf_op jit(solution)/shard_map/ppermute | solution.py:328
  72.1 0.9 collective-permute-start.24
  73.0 0.5 collective-permute-start.25
  73.5 0.9 collective-permute-start.26
  74.4 2.5 %collective-permute-start.28 = (bf16[288,256]{1,0:T(8,128)(2,1)S(1)}, bf16[288,256]{1,0:T(8,128)(2,1)S(1)}, u32[]{:S(2)}, u32[]{:S(2)}) collective-permute-start(bf16[288,256]{1,0:T(8,128)(2,1)S(1)} %get-tuple-element.112), channel_id=1, source_target_pairs={{0,128},{64,192},{128,0},{192,64},{1,129},{65,193},{129,1},{193,65... | collective-permute-start | bytes 442376 | tf_op jit(solution)/shard_map/ppermute | solution.py:328
  76.9 7.7 %collective-permute-done.27.k1_ref = bf16[288,256]{1,0:T(8,128)(2,1)S(1)} collective-permute-done((bf16[288,256]{1,0:T(8,128)(2,1)S(1)}, bf16[288,256]{1,0:T(8,128)(2,1)S(1)}, u32[]{:S(2)}, u32[]{:S(2)}) %collective-permute-start.27) | collective-permute-done | bytes 147488 | tf_op jit(solution)/shard_map/ppermute | solution.py:328
  84.6 4.4 %collective-permute-start.29 = (bf16[288,256]{1,0:T(8,128)(2,1)S(1)}, bf16[288,256]{1,0:T(8,128)(2,1)S(1)}, u32[]{:S(2)}, u32[]{:S(2)}) collective-permute-start(bf16[288,256]{1,0:T(8,128)(2,1)S(1)} %get-tuple-element.113), channel_id=1, source_target_pairs={{0,64},{64,128},{128,192},{192,0},{1,65},{65,129},{129,193},{193,1... | collective-permute-start | bytes 442376 | tf_op jit(solution)/shard_map/ppermute | solution.py:328
  89.0 1.4 %collective-permute-start.19 = (bf16[136,512]{1,0:T(8,128)(2,1)S(1)}, bf16[136,512]{1,0:T(8,128)(2,1)S(1)}, u32[]{:S(2)}, u32[]{:S(2)}) collective-permute-start(bf16[136,512]{1,0:T(8,128)(2,1)S(1)} %get-tuple-element.94), channel_id=1, source_target_pairs={{0,1},{1,2},{2,3},{3,0},{4,5},{5,6},{6,7},{7,4},{8,9},{9,10},{10,1... | collective-permute-start | bytes 417800 | tf_op jit(solution)/shard_map/ppermute | solution.py:328
  90.4 2.3 %collective-permute-done.29.k3_ref = bf16[288,256]{1,0:T(8,128)(2,1)S(1)} collective-permute-done((bf16[288,256]{1,0:T(8,128)(2,1)S(1)}, bf16[288,256]{1,0:T(8,128)(2,1)S(1)}, u32[]{:S(2)}, u32[]{:S(2)}) %collective-permute-start.29) | collective-permute-done | bytes 147488 | tf_op jit(solution)/shard_map/ppermute | solution.py:328
  92.8 2.6 %collective-permute-start.20 = (bf16[136,512]{1,0:T(8,128)(2,1)S(1)}, bf16[136,512]{1,0:T(8,128)(2,1)S(1)}, u32[]{:S(2)}, u32[]{:S(2)}) collective-permute-start(bf16[136,512]{1,0:T(8,128)(2,1)S(1)} %get-tuple-element.95), channel_id=1, source_target_pairs={{0,2},{1,3},{2,0},{3,1},{4,6},{5,7},{6,4},{7,5},{8,10},{9,11},{10,... | collective-permute-start | bytes 417800 | tf_op jit(solution)/shard_map/ppermute | solution.py:328
  95.4 0.1 ring.1
  95.5 1.9 %collective-permute-start.30 = (bf16[128,256]{1,0:T(8,128)(2,1)S(1)}, bf16[128,256]{1,0:T(8,128)(2,1)S(1)}, u32[]{:S(2)}, u32[]{:S(2)}) collective-permute-start(bf16[128,256]{1,0:T(8,128)(2,1)S(1)} %get-tuple-element.125), channel_id=1, source_target_pairs={{0,192},{64,128},{128,64},{192,0},{1,193},{65,129},{129,65},{193,1... | collective-permute-start | bytes 196616 | tf_op jit(solution)/shard_map/ppermute | solution.py:332
  97.5 4.5 %collective-permute-done.30.got_ref = bf16[128,256]{1,0:T(8,128)(2,1)S(1)} collective-permute-done((bf16[128,256]{1,0:T(8,128)(2,1)S(1)}, bf16[128,256]{1,0:T(8,128)(2,1)S(1)}, u32[]{:S(2)}, u32[]{:S(2)}) %collective-permute-start.30) | collective-permute-done | bytes 65568 | tf_op jit(solution)/shard_map/ppermute | solution.py:332
  102.0 3.6 %collective-permute-start.31 = (bf16[64,256]{1,0:T(8,128)(2,1)S(1)}, bf16[64,256]{1,0:T(8,128)(2,1)S(1)}, u32[]{:S(2)}, u32[]{:S(2)}) collective-permute-start(bf16[64,256]{1,0:T(8,128)(2,1)S(1)} %get-tuple-element.127), channel_id=1, source_target_pairs={{0,64},{64,0},{128,192},{192,128},{1,65},{65,1},{129,193},{193,129... | collective-permute-start | bytes 98312 | tf_op jit(solution)/shard_map/ppermute | solution.py:332
  105.6 2.1 %collective-permute-done.31.wgot_ref = bf16[64,256]{1,0:T(8,128)(2,1)S(1)} collective-permute-done((bf16[64,256]{1,0:T(8,128)(2,1)S(1)}, bf16[64,256]{1,0:T(8,128)(2,1)S(1)}, u32[]{:S(2)}, u32[]{:S(2)}) %collective-permute-start.31) | collective-permute-done | bytes 32800 | tf_op jit(solution)/shard_map/ppermute | solution.py:332
  107.7 0.1 total.1
  107.8 0.3 collective-permute-start.32
  108.1 0.7 add_convert_fusion
  108.8 3.9 %collective-permute-done.32.got_ref = bf16[496,128]{1,0:T(8,128)(2,1)S(1)} collective-permute-done((bf16[496,128]{1,0:T(8,128)(2,1)S(1)}, bf16[496,128]{1,0:T(8,128)(2,1)S(1)}, u32[]{:S(2)}, u32[]{:S(2)}) %collective-permute-start.32) | collective-permute-done | bytes 127008 | tf_op jit(solution)/shard_map/ppermute | solution.py:332
  112.8 1.3 %place.1 = (bf16[136,256]{1,0:T(8,128)(2,1)}, bf16[136,256]{1,0:T(8,128)(2,1)}, bf16[136,256]{1,0:T(8,128)(2,1)}, f32[32,256]{1,0:T(8,128)}) custom-call(s32[5]{0:T(128)S(1)} %stack.35.at_ref, bf16[144,384]{1,0:T(8,128)(2,1)S(1)} %get-tuple-element.128.mine_ref, f32[32,256]{1,0:T(8,128)S(1)} %get-tuple-element.129.wmine_ref, ...), custom_call_target="tpu_custom_call" | custom-call | tf_op jit(solution)/shard_map/place/pallas_call | solution.py:47
  (28 shorter events, 0.1 us)
Async XLA Ops:
  0.6 11.2 %copy-start = (bf16[256,2048]{1,0:T(8,128)(2,1)S(1)}, bf16[256,2048]{1,0:T(8,128)(2,1)}, u32[]{:S(2)}) copy-start(bf16[256,2048]{1,0:T(8,128)(2,1)} %param.10) | copy-start | bytes 3145732
  3.1 9.0 %collective-permute-start.3 = (bf16[144,256]{1,0:T(8,128)(2,1)S(1)}, bf16[144,256]{1,0:T(8,128)(2,1)S(1)}, u32[]{:S(2)}, u32[]{:S(2)}) collective-permute-start(bf16[144,256]{1,0:T(8,128)(2,1)S(1)} %get-tuple-element.70), channel_id=1, source_target_pairs={{0,32},{32,0},{1,33},{33,1},{2,34},{34,2},{3,35},{35,3},{4,36},{36... | collective-permute-start | bytes 221192 | tf_op jit(solution)/shard_map/ppermute | solution.py:332
  6.8 10.9 %collective-permute-start.2 = (bf16[136,512]{1,0:T(8,128)(2,1)S(1)}, bf16[136,512]{1,0:T(8,128)(2,1)S(1)}, u32[]{:S(2)}, u32[]{:S(2)}) collective-permute-start(bf16[136,512]{1,0:T(8,128)(2,1)S(1)} %broadcast_select_fusion.dy0_ref), channel_id=1, source_target_pairs={{0,3},{1,0},{2,1},{3,2},{4,7},{5,4},{6,5},{7,6},{8,11},{9,8},{10,9... | collective-permute-start | bytes 417800 | tf_op jit(solution)/shard_map/ppermute | solution.py:328
  7.3 10.3 %collective-permute-start.1 = (bf16[136,512]{1,0:T(8,128)(2,1)S(1)}, bf16[136,512]{1,0:T(8,128)(2,1)S(1)}, u32[]{:S(2)}, u32[]{:S(2)}) collective-permute-start(bf16[136,512]{1,0:T(8,128)(2,1)S(1)} %broadcast_select_fusion.dy0_ref), channel_id=1, source_target_pairs={{0,2},{1,3},{2,0},{3,1},{4,6},{5,7},{6,4},{7,5},{8,10},{9,11},{10,... | collective-permute-start | bytes 417800 | tf_op jit(solution)/shard_map/ppermute | solution.py:328
  9.9 7.8 %collective-permute-start = (bf16[136,512]{1,0:T(8,128)(2,1)S(1)}, bf16[136,512]{1,0:T(8,128)(2,1)S(1)}, u32[]{:S(2)}, u32[]{:S(2)}) collective-permute-start(bf16[136,512]{1,0:T(8,128)(2,1)S(1)} %broadcast_select_fusion.dy0_ref), channel_id=1, source_target_pairs={{0,1},{1,2},{2,3},{3,0},{4,5},{5,6},{6,7},{7,4},{8,9},{9,10},{10,1... | collective-permute-start | bytes 417800 | tf_op jit(solution)/shard_map/ppermute | solution.py:328
  12.1 19.1 %collective-permute-start.11 = (bf16[288,256]{1,0:T(8,128)(2,1)S(1)}, bf16[288,256]{1,0:T(8,128)(2,1)S(1)}, u32[]{:S(2)}, u32[]{:S(2)}) collective-permute-start(bf16[288,256]{1,0:T(8,128)(2,1)S(1)} %constant_dynamic-update-slice_fusion.refs_4_), channel_id=1, source_target_pairs={{0,4},{4,0},{1,5},{5,1},{2,6},{6,2},{3,7},{7,3},{8,12},{12,8},{9,1... | collective-permute-start | bytes 442376 | tf_op jit(solution)/shard_map/ppermute | solution.py:332
  12.2 19.8 %collective-permute-start.10 = (bf16[288,256]{1,0:T(8,128)(2,1)S(1)}, bf16[288,256]{1,0:T(8,128)(2,1)S(1)}, u32[]{:S(2)}, u32[]{:S(2)}) collective-permute-start(bf16[288,256]{1,0:T(8,128)(2,1)S(1)} %constant_dynamic-update-slice_fusion.refs_4_), channel_id=1, source_target_pairs={{0,192},{64,0},{128,64},{192,128},{1,193},{65,1},{129,65},{193,129... | collective-permute-start | bytes 442376 | tf_op jit(solution)/shard_map/ppermute | solution.py:328
  17.6 15.2 %collective-permute-start.8 = (bf16[288,256]{1,0:T(8,128)(2,1)S(1)}, bf16[288,256]{1,0:T(8,128)(2,1)S(1)}, u32[]{:S(2)}, u32[]{:S(2)}) collective-permute-start(bf16[288,256]{1,0:T(8,128)(2,1)S(1)} %constant_dynamic-update-slice_fusion.refs_4_), channel_id=1, source_target_pairs={{0,64},{64,128},{128,192},{192,0},{1,65},{65,129},{129,193},{193,1... | collective-permute-start | bytes 442376 | tf_op jit(solution)/shard_map/ppermute | solution.py:328
  18.7 9.7 %collective-permute-start.4 = (bf16[144,256]{1,0:T(8,128)(2,1)S(1)}, bf16[144,256]{1,0:T(8,128)(2,1)S(1)}, u32[]{:S(2)}, u32[]{:S(2)}) collective-permute-start(bf16[144,256]{1,0:T(8,128)(2,1)S(1)} %get-tuple-element.78), channel_id=1, source_target_pairs={{0,32},{32,0},{1,33},{33,1},{2,34},{34,2},{3,35},{35,3},{4,36},{36... | collective-permute-start | bytes 221192 | tf_op jit(solution)/shard_map/ppermute | solution.py:332
  19.8 14.3 %collective-permute-start.9 = (bf16[288,256]{1,0:T(8,128)(2,1)S(1)}, bf16[288,256]{1,0:T(8,128)(2,1)S(1)}, u32[]{:S(2)}, u32[]{:S(2)}) collective-permute-start(bf16[288,256]{1,0:T(8,128)(2,1)S(1)} %constant_dynamic-update-slice_fusion.refs_4_), channel_id=1, source_target_pairs={{0,128},{64,192},{128,0},{192,64},{1,129},{65,193},{129,1},{193,65... | collective-permute-start | bytes 442376 | tf_op jit(solution)/shard_map/ppermute | solution.py:328
  28.4 9.1 %collective-permute-start.7 = (bf16[288,256]{1,0:T(8,128)(2,1)S(1)}, bf16[288,256]{1,0:T(8,128)(2,1)S(1)}, u32[]{:S(2)}, u32[]{:S(2)}) collective-permute-start(bf16[288,256]{1,0:T(8,128)(2,1)S(1)} %constant_dynamic-update-slice_fusion.2.refs_0_), channel_id=1, source_target_pairs={{0,24},{8,0},{16,8},{24,16},{1,25},{9,1},{17,9},{25,17},{2,26},{10... | collective-permute-start | bytes 442376 | tf_op jit(solution)/shard_map/ppermute | solution.py:328
  31.2 8.3 %collective-permute-start.6 = (bf16[288,256]{1,0:T(8,128)(2,1)S(1)}, bf16[288,256]{1,0:T(8,128)(2,1)S(1)}, u32[]{:S(2)}, u32[]{:S(2)}) collective-permute-start(bf16[288,256]{1,0:T(8,128)(2,1)S(1)} %constant_dynamic-update-slice_fusion.2.refs_0_), channel_id=1, source_target_pairs={{0,16},{8,24},{16,0},{24,8},{1,17},{9,25},{17,1},{25,9},{2,18},{10... | collective-permute-start | bytes 442376 | tf_op jit(solution)/shard_map/ppermute | solution.py:328
  32.0 9.3 %collective-permute-start.5 = (bf16[288,256]{1,0:T(8,128)(2,1)S(1)}, bf16[288,256]{1,0:T(8,128)(2,1)S(1)}, u32[]{:S(2)}, u32[]{:S(2)}) collective-permute-start(bf16[288,256]{1,0:T(8,128)(2,1)S(1)} %constant_dynamic-update-slice_fusion.2.refs_0_), channel_id=1, source_target_pairs={{0,8},{8,16},{16,24},{24,0},{1,9},{9,17},{17,25},{25,1},{2,10},{10... | collective-permute-start | bytes 442376 | tf_op jit(solution)/shard_map/ppermute | solution.py:328
  32.9 8.4 %collective-permute-start.14 = (bf16[288,256]{1,0:T(8,128)(2,1)S(1)}, bf16[288,256]{1,0:T(8,128)(2,1)S(1)}, u32[]{:S(2)}, u32[]{:S(2)}) collective-permute-start(bf16[288,256]{1,0:T(8,128)(2,1)S(1)} %collective-permute-done.10.refs_7_), channel_id=1, source_target_pairs={{0,4},{4,0},{1,5},{5,1},{2,6},{6,2},{3,7},{7,3},{8,12},{12,8},{9,1... | collective-permute-start | bytes 442376 | tf_op jit(solution)/shard_map/ppermute | solution.py:332
  34.1 7.2 %collective-permute-start.12 = (bf16[288,256]{1,0:T(8,128)(2,1)S(1)}, bf16[288,256]{1,0:T(8,128)(2,1)S(1)}, u32[]{:S(2)}, u32[]{:S(2)}) collective-permute-start(bf16[288,256]{1,0:T(8,128)(2,1)S(1)} %collective-permute-done.8.refs_5_), channel_id=1, source_target_pairs={{0,4},{4,0},{1,5},{5,1},{2,6},{6,2},{3,7},{7,3},{8,12},{12,8},{9,1... | collective-permute-start | bytes 442376 | tf_op jit(solution)/shard_map/ppermute | solution.py:332
  37.5 3.7 %collective-permute-start.13 = (bf16[288,256]{1,0:T(8,128)(2,1)S(1)}, bf16[288,256]{1,0:T(8,128)(2,1)S(1)}, u32[]{:S(2)}, u32[]{:S(2)}) collective-permute-start(bf16[288,256]{1,0:T(8,128)(2,1)S(1)} %collective-permute-done.9.refs_6_), channel_id=1, source_target_pairs={{0,4},{4,0},{1,5},{5,1},{2,6},{6,2},{3,7},{7,3},{8,12},{12,8},{9,1... | collective-permute-start | bytes 442376 | tf_op jit(solution)/shard_map/ppermute | solution.py:332
  46.2 5.6 %collective-permute-start.15 = (bf16[368,128]{1,0:T(8,128)(2,1)S(1)}, bf16[368,128]{1,0:T(8,128)(2,1)S(1)}, u32[]{:S(2)}, u32[]{:S(2)}) collective-permute-start(bf16[368,128]{1,0:T(8,128)(2,1)S(1)} %get-tuple-element.81), channel_id=1, source_target_pairs={{0,24},{8,0},{16,8},{24,16},{1,25},{9,1},{17,9},{25,17},{2,26},{10... | collective-permute-start | bytes 282632 | tf_op jit(solution)/shard_map/ppermute | solution.py:328
  47.6 7.0 %collective-permute-start.16 = (bf16[368,128]{1,0:T(8,128)(2,1)S(1)}, bf16[368,128]{1,0:T(8,128)(2,1)S(1)}, u32[]{:S(2)}, u32[]{:S(2)}) collective-permute-start(bf16[368,128]{1,0:T(8,128)(2,1)S(1)} %get-tuple-element.82), channel_id=1, source_target_pairs={{0,16},{8,24},{16,0},{24,8},{1,17},{9,25},{17,1},{25,9},{2,18},{10... | collective-permute-start | bytes 282632 | tf_op jit(solution)/shard_map/ppermute | solution.py:328
  47.7 7.7 %collective-permute-start.17 = (bf16[368,128]{1,0:T(8,128)(2,1)S(1)}, bf16[368,128]{1,0:T(8,128)(2,1)S(1)}, u32[]{:S(2)}, u32[]{:S(2)}) collective-permute-start(bf16[368,128]{1,0:T(8,128)(2,1)S(1)} %get-tuple-element.83), channel_id=1, source_target_pairs={{0,8},{8,16},{16,24},{24,0},{1,9},{9,17},{17,25},{25,1},{2,10},{10... | collective-permute-start | bytes 282632 | tf_op jit(solution)/shard_map/ppermute | solution.py:328
  60.3 9.8 %collective-permute-start.22 = (bf16[4,288,256]{2,1,0:T(8,128)(2,1)S(1)}, bf16[4,288,256]{2,1,0:T(8,128)(2,1)S(1)}, u32[]{:S(2)}, u32[]{:S(2)}) collective-permute-start(bf16[4,288,256]{2,1,0:T(8,128)(2,1)S(1)} %get-tuple-element.101), channel_id=1, source_target_pairs={{0,4},{4,0},{1,5},{5,1},{2,6},{6,2},{3,7},{7,3},{8,12},{12,8},{9,1... | collective-permute-start | bytes 1769480 | tf_op jit(solution)/shard_map/ppermute | solution.py:332
  60.4 4.3 %collective-permute-start.18 = (bf16[144,128]{1,0:T(8,128)(2,1)S(1)}, bf16[144,128]{1,0:T(8,128)(2,1)S(1)}, u32[]{:S(2)}, u32[]{:S(2)}) collective-permute-start(bf16[144,128]{1,0:T(8,128)(2,1)S(1)} %get-tuple-element.85), channel_id=1, source_target_pairs={{0,32},{32,0},{1,33},{33,1},{2,34},{34,2},{3,35},{35,3},{4,36},{36... | collective-permute-start | bytes 110600 | tf_op jit(solution)/shard_map/ppermute | solution.py:332
  65.9 4.2 %collective-permute-start.23 = (bf16[4,256,256]{2,1,0:T(8,128)(2,1)S(1)}, bf16[4,256,256]{2,1,0:T(8,128)(2,1)S(1)}, u32[]{:S(2)}, u32[]{:S(2)}) collective-permute-start(bf16[4,256,256]{2,1,0:T(8,128)(2,1)S(1)} %get-tuple-element.103), channel_id=1, source_target_pairs={{0,4},{4,0},{1,5},{5,1},{2,6},{6,2},{3,7},{7,3},{8,12},{12,8},{9,1... | collective-permute-start | bytes 1572872 | tf_op jit(solution)/shard_map/ppermute | solution.py:332
  70.3 14.3 %collective-permute-start.27 = (bf16[288,256]{1,0:T(8,128)(2,1)S(1)}, bf16[288,256]{1,0:T(8,128)(2,1)S(1)}, u32[]{:S(2)}, u32[]{:S(2)}) collective-permute-start(bf16[288,256]{1,0:T(8,128)(2,1)S(1)} %get-tuple-element.111), channel_id=1, source_target_pairs={{0,192},{64,0},{128,64},{192,128},{1,193},{65,1},{129,65},{193,129... | collective-permute-start | bytes 442376 | tf_op jit(solution)/shard_map/ppermute | solution.py:328
  72.1 23.3 %collective-permute-start.24 = (bf16[800,128]{1,0:T(8,128)(2,1)S(1)}, bf16[800,128]{1,0:T(8,128)(2,1)S(1)}, u32[]{:S(2)}, u32[]{:S(2)}) collective-permute-start(bf16[800,128]{1,0:T(8,128)(2,1)S(1)} %get-tuple-element.107), channel_id=1, source_target_pairs={{0,24},{8,0},{16,8},{24,16},{1,25},{9,1},{17,9},{25,17},{2,26},{10... | collective-permute-start | bytes 614408 | tf_op jit(solution)/shard_map/ppermute | solution.py:328
  73.0 22.4 %collective-permute-start.25 = (bf16[800,128]{1,0:T(8,128)(2,1)S(1)}, bf16[800,128]{1,0:T(8,128)(2,1)S(1)}, u32[]{:S(2)}, u32[]{:S(2)}) collective-permute-start(bf16[800,128]{1,0:T(8,128)(2,1)S(1)} %get-tuple-element.108), channel_id=1, source_target_pairs={{0,16},{8,24},{16,0},{24,8},{1,17},{9,25},{17,1},{25,9},{2,18},{10... | collective-permute-start | bytes 614408 | tf_op jit(solution)/shard_map/ppermute | solution.py:328
  73.5 21.9 %collective-permute-start.26 = (bf16[800,128]{1,0:T(8,128)(2,1)S(1)}, bf16[800,128]{1,0:T(8,128)(2,1)S(1)}, u32[]{:S(2)}, u32[]{:S(2)}) collective-permute-start(bf16[800,128]{1,0:T(8,128)(2,1)S(1)} %get-tuple-element.109), channel_id=1, source_target_pairs={{0,8},{8,16},{16,24},{24,0},{1,9},{9,17},{17,25},{25,1},{2,10},{10... | collective-permute-start | bytes 614408 | tf_op jit(solution)/shard_map/ppermute | solution.py:328
  74.4 14.6 %collective-permute-start.28 = (bf16[288,256]{1,0:T(8,128)(2,1)S(1)}, bf16[288,256]{1,0:T(8,128)(2,1)S(1)}, u32[]{:S(2)}, u32[]{:S(2)}) collective-permute-start(bf16[288,256]{1,0:T(8,128)(2,1)S(1)} %get-tuple-element.112), channel_id=1, source_target_pairs={{0,128},{64,192},{128,0},{192,64},{1,129},{65,193},{129,1},{193,65... | collective-permute-start | bytes 442376 | tf_op jit(solution)/shard_map/ppermute | solution.py:328
  84.6 8.1 %collective-permute-start.29 = (bf16[288,256]{1,0:T(8,128)(2,1)S(1)}, bf16[288,256]{1,0:T(8,128)(2,1)S(1)}, u32[]{:S(2)}, u32[]{:S(2)}) collective-permute-start(bf16[288,256]{1,0:T(8,128)(2,1)S(1)} %get-tuple-element.113), channel_id=1, source_target_pairs={{0,64},{64,128},{128,192},{192,0},{1,65},{65,129},{129,193},{193,1... | collective-permute-start | bytes 442376 | tf_op jit(solution)/shard_map/ppermute | solution.py:328
  89.0 19.1 %collective-permute-start.19 = (bf16[136,512]{1,0:T(8,128)(2,1)S(1)}, bf16[136,512]{1,0:T(8,128)(2,1)S(1)}, u32[]{:S(2)}, u32[]{:S(2)}) collective-permute-start(bf16[136,512]{1,0:T(8,128)(2,1)S(1)} %get-tuple-element.94), channel_id=1, source_target_pairs={{0,1},{1,2},{2,3},{3,0},{4,5},{5,6},{6,7},{7,4},{8,9},{9,10},{10,1... | collective-permute-start | bytes 417800 | tf_op jit(solution)/shard_map/ppermute | solution.py:328
  92.8 15.3 %collective-permute-start.20 = (bf16[136,512]{1,0:T(8,128)(2,1)S(1)}, bf16[136,512]{1,0:T(8,128)(2,1)S(1)}, u32[]{:S(2)}, u32[]{:S(2)}) collective-permute-start(bf16[136,512]{1,0:T(8,128)(2,1)S(1)} %get-tuple-element.95), channel_id=1, source_target_pairs={{0,2},{1,3},{2,0},{3,1},{4,6},{5,7},{6,4},{7,5},{8,10},{9,11},{10,... | collective-permute-start | bytes 417800 | tf_op jit(solution)/shard_map/ppermute | solution.py:328
  95.4 12.7 %collective-permute-start.21 = (bf16[136,512]{1,0:T(8,128)(2,1)S(1)}, bf16[136,512]{1,0:T(8,128)(2,1)S(1)}, u32[]{:S(2)}, u32[]{:S(2)}) collective-permute-start(bf16[136,512]{1,0:T(8,128)(2,1)S(1)} %get-tuple-element.96), channel_id=1, source_target_pairs={{0,3},{1,0},{2,1},{3,2},{4,7},{5,4},{6,5},{7,6},{8,11},{9,8},{10,9... | collective-permute-start | bytes 417800 | tf_op jit(solution)/shard_map/ppermute | solution.py:328
  95.5 6.5 %collective-permute-start.30 = (bf16[128,256]{1,0:T(8,128)(2,1)S(1)}, bf16[128,256]{1,0:T(8,128)(2,1)S(1)}, u32[]{:S(2)}, u32[]{:S(2)}) collective-permute-start(bf16[128,256]{1,0:T(8,128)(2,1)S(1)} %get-tuple-element.125), channel_id=1, source_target_pairs={{0,192},{64,128},{128,64},{192,0},{1,193},{65,129},{129,65},{193,1... | collective-permute-start | bytes 196616 | tf_op jit(solution)/shard_map/ppermute | solution.py:332
  102.0 5.7 %collective-permute-start.31 = (bf16[64,256]{1,0:T(8,128)(2,1)S(1)}, bf16[64,256]{1,0:T(8,128)(2,1)S(1)}, u32[]{:S(2)}, u32[]{:S(2)}) collective-permute-start(bf16[64,256]{1,0:T(8,128)(2,1)S(1)} %get-tuple-element.127), channel_id=1, source_target_pairs={{0,64},{64,0},{128,192},{192,128},{1,65},{65,1},{129,193},{193,129... | collective-permute-start | bytes 98312 | tf_op jit(solution)/shard_map/ppermute | solution.py:332
  107.8 5.0 %collective-permute-start.32 = (bf16[496,128]{1,0:T(8,128)(2,1)S(1)}, bf16[496,128]{1,0:T(8,128)(2,1)S(1)}, u32[]{:S(2)}, u32[]{:S(2)}) collective-permute-start(bf16[496,128]{1,0:T(8,128)(2,1)S(1)} %get-tuple-element.130), channel_id=1, source_target_pairs={{0,32},{32,0},{1,33},{33,1},{2,34},{34,2},{3,35},{35,3},{4,36},{36... | collective-permute-start | bytes 380936 | tf_op jit(solution)/shard_map/ppermute | solution.py:332

commit v2 on v1

--- a/solution.py
+++ b/solution.py
@@ -67,38 +67,49 @@
         send_ref[...] = first
 
 
-def pack_kernel(at_ref, qkv_ref, ids_ref, keep_ref, send_ref, qkeep_ref, qsend_ref):
+def pack_kernel(at_ref, all_ref, ids_ref, keep_ref, send_ref, qkeep_ref, qsend_ref, dy_ref):
     ids = ids_ref[...].astype(BF16)
     zero = jnp.zeros((8, DH), BF16)
     kvs, qs = [], []
     for head in range(2):
-        cols = slice(head * DH, (head + 1) * DH)
-        k = jnp.concatenate([qkv_ref[1, :, cols], ids], axis=0)
-        v = jnp.concatenate([qkv_ref[2, :, cols], zero], axis=0)
-        kvs.append(jnp.concatenate([k, v], axis=1))
-        qs.append(jnp.concatenate([qkv_ref[0, :, cols], ids], axis=0))
+        q, k, v = (all_ref[:, i * FEATS + head * DH : i * FEATS + (head + 1) * DH] for i in range(3))
+        kvs.append(jnp.concatenate([k, ids, v, zero], axis=0))
+        qs.append(jnp.concatenate([q, ids], axis=0))
     by_parity(at_ref[0], kvs[0], kvs[1], keep_ref, send_ref)
     by_parity(at_ref[0], qs[0], qs[1], qkeep_ref, qsend_ref)
-
-
-def dattn_kernel(at_ref, dy0_ref, dy1_ref, dy2_ref, dy3_ref, wo_ref, qkeep_ref, qsend_ref, keep_ref, send_ref):
+    dy_ref[...] = all_ref[:, 3 * FEATS : 3 * FEATS + WIDE]
+
+
+def dattn_kernel(at_ref, *refs):
+    dy_refs, (wo_ref, ids_ref, qkeep_ref, qsend_ref, keep_ref, send_ref) = refs[0:4], refs[4:]
     acc = jnp.zeros((ROWS, FEATS), F32)
-    for s, ref in enumerate((dy0_ref, dy1_ref, dy2_ref, dy3_ref)):
+    for s, ref in enumerate(dy_refs):
         block = wo_ref[:, s * WIDE : (s + 1) * WIDE]
         acc = acc + lax.dot_general(ref[...], block, LAST, preferred_element_type=F32)
-    acc = jnp.concatenate([acc.astype(BF16), jnp.zeros((PAD - ROWS, FEATS), BF16)], axis=0)
-    keep_ref[:, 0:DH] = qkeep_ref[...]
-    send_ref[:, 0:DH] = qsend_ref[...]
-    by_parity(at_ref[0], acc[:, 0:DH], acc[:, DH:FEATS], keep_ref.at[:, DH:FEATS], send_ref.at[:, DH:FEATS])
-
-
-def assemble(pair_refs, all_ref, base):
+    ids = ids_ref[...].T
+    real = jnp.concatenate([ids[:, 0:1], ids[0:8, 1:2]], axis=0) >= 0.0
+    acc = jnp.where(real, acc, 0.0).astype(BF16)
+    acc = jnp.concatenate([acc, jnp.zeros((PAD - ROWS, FEATS), BF16)], axis=0)
+    keep_ref[0:PAD] = qkeep_ref[...]
+    send_ref[0:PAD] = qsend_ref[...]
+    by_parity(at_ref[0], acc[:, 0:DH], acc[:, DH:FEATS], keep_ref.at[PAD:PAIR], send_ref.at[PAD:PAIR])
+
+
+def pairs_of(refs, slots):
+    found = [None] * 4
+    for i, slot in enumerate(slots):
+        found[slot] = (refs[i // 2], i % 2 * PAIR)
+    return found
+
+
+def assemble(pairs, all_ref, base, cols):
     rest = base + QREST
-    for j, ref in enumerate(pair_refs):
+    for j, (ref, at) in enumerate(pairs):
         for k in range(2):
             half = 2 * j + k
-            all_ref[base + half * FINE : base + (half + 1) * FINE] = ref[k * PAD : k * PAD + FINE]
-            all_ref[rest + half * REST : rest + (half + 1) * REST] = ref[k * PAD + FINE : (k + 1) * PAD]
+            top = at + k * PAD
+            all_ref[base + half * FINE : base + (half + 1) * FINE, cols] = ref[top : top + FINE]
+            all_ref[rest + half * REST : rest + (half + 1) * REST, cols] = ref[top + FINE : top + PAD]
 
 
 def take_pair(value, j):
@@ -109,11 +120,11 @@
     return jnp.concatenate(pieces, axis=0)
 
 
-def masks(pair_refs, mask_ref, base, is_query):
+def masks(pairs, mask_ref, base, is_query):
     fine, last = [], []
-    for ref in pair_refs:
+    for ref, at in pairs:
         for k in range(2):
-            rows = ref[k * PAD + FINE : (k + 1) * PAD, 0:DH].astype(F32)
+            rows = ref[at + k * PAD + FINE : at + (k + 1) * PAD].astype(F32)
             fine.append(rows[8:9])
             last.append(rows[9:10])
     fine = jnp.concatenate(fine, axis=0).T
@@ -127,7 +138,7 @@
             return jnp.where(hidden, BIG, 0.0).astype(BF16)
         return jnp.where(lane == jnp.where(column < 0.0, 13.0, column), 1.0, 0.0).astype(BF16)
 
-    for half in range(2 * len(pair_refs)):
+    for half in range(2 * len(pairs)):
         mask_ref[base + half * FINE : base + (half + 1) * FINE] = encode(fine[:, half : half + 1])
         mask_ref[rest + half * REST : rest + (half + 1) * REST] = encode(last[0:REST, half : half + 1])
 
@@ -139,13 +150,17 @@
 
 
 def forward_kernel(*refs):
-    q_parts, kv_parts = refs[0:4], refs[4:12]
     load_refs, q_ref, qm_ref, kv_ref, km_ref, o_ref, stat_ref = refs[12:16], *refs[16:22]
-    assemble(q_parts, q_ref, 0)
-    masks(q_parts, qm_ref, 0, True)
-    for base, parts in ((0, kv_parts[0:4]), (NQ, kv_parts[4:8])):
-        assemble(parts, kv_ref, base)
-        masks(parts, km_ref, base, False)
+    left, right = slice(0, DH), slice(DH, FEATS)
+    queries = pairs_of(refs[0:2], (0, 1, 3, 2))
+    assemble(queries, q_ref, 0, left)
+    assemble(pairs_of(refs[2:4], (0, 3, 1, 2)), q_ref, 0, right)
+    masks(queries, qm_ref, 0, True)
+    for base, parts in ((0, refs[4:8]), (NQ, refs[8:12])):
+        keys = pairs_of(parts[0:2], (0, 1, 3, 2))
+        assemble(keys, kv_ref, base, left)
+        assemble(pairs_of(parts[2:4], (0, 3, 1, 2)), kv_ref, base, right)
+        masks(keys, km_ref, base, False)
     k_ext = jnp.concatenate([kv_ref[:, 0:DH], km_ref[...]], axis=1)
     lane = lax.broadcasted_iota(jnp.int32, (BLOCK, DH), 1)
     for block in range(NQ // BLOCK):
@@ -172,12 +187,16 @@
 
 def row_sums(load_refs):
     lses, shares = [], []
+    odd = lax.broadcasted_iota(jnp.int32, (8, DH), 1) % (4 * REST) >= 2 * REST
     for s, ref in enumerate(load_refs):
         sums = ref[PAIR:LOAD].astype(F32)
         tiles = [sums[8 * i : 8 * i + 8] for i in range(9)]
-        last = tiles[8] if s == 0 else pltpu.roll(tiles[8], FINE - 2 * REST * s, 1)
-        order = [tiles[2 * ((j + s) % 4) + k] for j in range(4) for k in range(2)] + [last]
-        rows = jnp.concatenate(order, axis=1)
+        last = tiles[8]
+        if s % 2 == 1:
+            last = jnp.where(odd, pltpu.roll(last, 2 * REST, 1), pltpu.roll(last, FINE - 2 * REST, 1))
+        if s >= 2:
+            last = pltpu.roll(last, FINE // 2, 1)
+        rows = jnp.concatenate([tiles[2 * (j ^ s) + k] for j in range(4) for k in range(2)] + [last], axis=1)
         lses.append(rows[0:1] + rows[1:2] + rows[2:3])
         shares.append(rows[3:4] + rows[4:5] + rows[5:6])
     top = jnp.maximum(jnp.maximum(lses[0], lses[1]), jnp.maximum(lses[2], lses[3]))
@@ -209,15 +228,18 @@
         dkv_ref[rows, 0:DH] = (jnp.dot(ds, q, preferred_element_type=F32) * SCALE).astype(BF16)
         ds_ref[rows] = ds
     for j in range(4):
-        dkv_out_ref[j] = take_pair(dkv_ref, j)
+        pair = take_pair(dkv_ref, j)
+        dkv_out_ref[j] = pair[:, 0:DH]
+        dkv_out_ref[4 + j] = pair[:, DH:FEATS]
     keys = slice(base, base + NQ)
     dq = lax.dot_general(ds_ref[...], kv_ref[keys, 0:DH], FIRST, preferred_element_type=F32)
     if base > 0:
         dq_refs[0][...] = dq
     else:
-        dq = ((dq + dq_in_ref[...]) * SCALE).astype(BF16)
-        for j in range(4):
-            dq_refs[j][...] = take_pair(dq, j)
+        dq = (dq + dq_in_ref[...]) * SCALE
+        for at, (mine, theirs) in enumerate(((0, 1), (3, 2))):
+            dq_refs[0][at * PAIR : (at + 1) * PAIR] = take_pair(dq, mine)
+            dq_refs[1][at * PAIR : (at + 1) * PAIR] = take_pair(dq, theirs).astype(BF16)
 
 
 def merge_kernel(l0_ref, l1_ref, l2_ref, l3_ref, keep_ref, send_ref):
@@ -260,31 +282,38 @@
         for et in range(2):
             for t in range(4):
                 s = lax.rem(h - jnp.bitwise_xor(zr, t) + NH, NH)
-                row = lax.rem(e + et, 2) * 256 + lax.rem(x + xt, 4) * 64
+                row = lax.rem(e + et, 2) * 256 + jnp.bitwise_xor(x, xt) * 64
                 to = slice((et * 4 + t) * COLS, (et * 4 + t + 1) * COLS)
                 keep_ref[xt, to] = dwo_ref[s, pl.ds(pl.multiple_of(row + c * COLS, COLS), COLS)]
                 send_ref[xt, to] = dwo_ref[s, pl.ds(pl.multiple_of(row + (1 - c) * COLS, COLS), COLS)]
 
 
-def core_kernel(keep_ref, got_ref, wkeep_ref, wgot_ref, dq1_ref, dq2_ref, dq3_ref, *refs):
-    mine_ref, z_refs, wmine_ref, x_refs = refs[0], refs[1:4], refs[4], refs[5:8]
+def split_up(total, mine, theirs, keep_ref, send_ref):
+    rows = total.shape[1]
+    for at in range(len(mine)):
+        keep_ref[at * rows : (at + 1) * rows] = total[mine[at]]
+        send_ref[at * rows : (at + 1) * rows] = total[theirs[at]].astype(BF16)
+
+
+def core_kernel(keep_ref, got_ref, wkeep_ref, wgot_ref, *refs):
     total = keep_ref[...].astype(F32) + got_ref[...].astype(F32)
-    mine_ref[...] = total[0]
+    split_up(total[0:4], (0, 3), (1, 2), refs[0], refs[1])
+    split_up(total[4:8], (0, 1), (3, 2), refs[2], refs[3])
     weights = wkeep_ref[...].astype(F32) + wgot_ref[...].astype(F32)
-    wmine_ref[...] = weights[0]
-    for s, dq_ref in ((1, dq1_ref), (2, dq2_ref), (3, dq3_ref)):
-        z_refs[s - 1][...] = total[s].astype(BF16)
-        piece = weights[4 - s].astype(BF16)
-        x_refs[s - 1][0:PAIR] = dq_ref[...]
-        x_refs[s - 1][PAIR : PAIR + 256] = piece[:, 0:DH]
-        x_refs[s - 1][PAIR + 256 : PAIR + 512] = piece[:, DH:FEATS]
-
-
-def ring_kernel(dq0_ref, wmine_ref, x1_ref, x2_ref, x3_ref, dq_ref, keep_ref, send_ref):
-    got = [ref[...].astype(F32) for ref in (x1_ref, x2_ref, x3_ref)]
-    got = got[0] + got[1] + got[2]
-    dq_ref[...] = dq0_ref[...].astype(F32) + got[0:PAIR]
-    total = wmine_ref[...] + jnp.concatenate([got[PAIR : PAIR + 256], got[PAIR + 256 : PAIR + 512]], axis=1)
+    split_up(weights, (0, 1), (3, 2), refs[4], refs[5])
+
+
+def middle_kernel(*refs):
+    for i in range(4):
+        keep_ref, got_ref, mine_ref, send_ref = refs[2 * i], refs[2 * i + 1], refs[8 + 2 * i], refs[9 + 2 * i]
+        rows = mine_ref.shape[0]
+        total = keep_ref[...] + got_ref[...].astype(F32)
+        mine_ref[...] = total[0:rows]
+        send_ref[...] = total[rows : 2 * rows].astype(BF16)
+
+
+def ring_kernel(mine_ref, got_ref, keep_ref, send_ref):
+    total = mine_ref[...] + got_ref[...].astype(F32)
     for et in range(2):
         at = et * 4 * COLS
         to = et * 2 * COLS
@@ -300,12 +329,12 @@
         send_ref[et * COLS : (et + 1) * COLS] = total[(et * 2 + 1) * COLS : (et * 2 + 2) * COLS].astype(BF16)
 
 
-def total_kernel(k0_ref, k1_ref, k2_ref, k3_ref, dq_ref, wkeep_ref, wgot_ref, keep_ref, wmine_ref, send_ref):
-    dkv = k0_ref[...] + sum(ref[...].astype(F32) for ref in (k1_ref, k2_ref, k3_ref))
-    both = jnp.concatenate([dq_ref[...], dkv], axis=1).astype(BF16)
-    keep_ref[...] = both[0:PAD]
+def total_kernel(*refs):
+    wkeep_ref, wgot_ref, keep_ref, wmine_ref, send_ref = refs[6:11]
     for i in range(3):
-        send_ref[i * PAD : (i + 1) * PAD] = both[PAD:PAIR, i * DH : (i + 1) * DH]
+        total = (refs[2 * i][...] + refs[2 * i + 1][...].astype(F32)).astype(BF16)
+        keep_ref[:, i * DH : (i + 1) * DH] = total[0:PAD]
+        send_ref[i * PAD : (i + 1) * PAD] = total[PAD:PAIR]
     weights = wkeep_ref[...] + wgot_ref[...].astype(F32)
     wmine_ref[...] = weights[0:COLS]
     piece = weights[COLS : 2 * COLS].astype(BF16)
@@ -336,44 +365,50 @@
     return [value] + [shifted(value, axis, 4, s) for s in (1, 2, 3)]
 
 
+def doubled(value, axis, first, second):
+    near = jnp.concatenate([value, swapped(value, axis, 4, first)], axis=0)
+    return [near, swapped(near, axis, 4, second)]
+
+
 def local(queries, key_rows, value_rows, scale_of, wo, dy):
     axes = ("e", "head", "zr", "x", "c")
     at = jnp.stack([lax.axis_index(name) for name in axes]).astype(jnp.int32)
     ids = jnp.pad(scale_of, (0, 8 * DH - ROWS), constant_values=-1).reshape(8, DH).astype(F32)
-    pair = (PAIR, FEATS)
-
-    keep, send, qkeep, qsend = call(
+    pair = (PAIR, DH)
+
+    keep, send, qkeep, qsend, dy = call(
         pack_kernel,
         "pack",
-        [at, jnp.stack([queries, key_rows, value_rows]), ids],
-        [shape((PAD, FEATS))] * 2 + [shape((PAD, DH))] * 2,
+        [at, jnp.concatenate([queries, key_rows, value_rows, dy], axis=1), ids],
+        [shape(pair)] * 2 + [shape((PAD, DH))] * 2 + [shape((ROWS, WIDE))],
         scalars=1,
     )
-    kv = jnp.concatenate([keep, swapped(send, "e", 2, 1)], axis=0)
+    got = swapped(send, "e", 2, 1)
     dy, send = lax.optimization_barrier((dy, send))
-    dys = around(jnp.where(scale_of[:, None] >= 0, dy, 0), "head")
-    wo, _ = lax.optimization_barrier((wo, dys[0]))
+    ks = doubled(jnp.concatenate([keep[0:PAD], got[0:PAD]], axis=0), "zr", 1, 3)
+    vs = doubled(jnp.concatenate([keep[PAD:PAIR], got[PAD:PAIR]], axis=0), "zr", 3, 1)
+    dys = around(dy, "head")
+    wo, _ = lax.optimization_barrier((wo, dy))
     at_head = lax.axis_index("head")
     wo = jnp.concatenate(
         [lax.dynamic_slice_in_dim(wo, lax.rem(at_head - s + NH, NH) * WIDE, WIDE, 1) for s in range(NH)], axis=1
     )
-    keep, send = call(
-        dattn_kernel, "dattn", [at, *dys, wo, qkeep, qsend], [shape((PAD, FEATS))] * 2, scalars=1
-    )
-    kv_late, send = lax.optimization_barrier((kv, send))
-    kvs = [kv, shifted(kv, "zr", 4, 1), shifted(kv_late, "zr", 4, 2), shifted(kv, "zr", 4, 3)]
-    qs = around(jnp.concatenate([keep, swapped(send, "e", 2, 1)], axis=0), "x")
+    keep, send = call(dattn_kernel, "dattn", [at, *dys, wo, ids, qkeep, qsend], [shape(pair)] * 2, scalars=1)
+    got = swapped(send, "e", 2, 1)
+    qs = doubled(jnp.concatenate([keep[0:PAD], got[0:PAD]], axis=0), "x", 1, 3)
+    das = doubled(jnp.concatenate([keep[PAD:PAIR], got[PAD:PAIR]], axis=0), "x", 3, 1)
+    kvs = ks + vs
     kvs = kvs + [swapped(one, "c", 2, 1) for one in kvs]
 
     *loads, q, qm, kv, km = call(
         forward_kernel,
         "forward",
-        [*qs, *kvs],
+        [*qs, *das, *kvs],
         [shape((LOAD, DH))] * 4 + [shape((NQ, FEATS)), shape((NQ, DH)), shape((NK, FEATS)), shape((NK, DH))],
         [pltpu.VMEM((NQ, DH), BF16), pltpu.VMEM((8, NQ), F32)],
         flops=6 * NQ * NK * DH,
     )
-    loads = [loads[0]] + [shifted(loads[s], "x", 4, -s) for s in (1, 2, 3)]
+    loads = [loads[0]] + [swapped(loads[s], "x", 4, s) for s in (1, 2, 3)]
 
     keep, send = call(merge_kernel, "merge", loads, [shape((PAD, DH))] * 2)
     other = swapped(send, "e", 2, 1)
@@ -383,7 +418,7 @@
         functools.partial(backward_kernel, NQ),
         "backward_far",
         [q, qm, kv, km, *loads],
-        [shape((4, *pair)), shape((NQ, DH), F32)],
+        [shape((8, *pair)), shape((NQ, DH), F32)],
         scratch,
         flops=6 * NQ * NK * DH,
     )
@@ -397,28 +432,38 @@
         scalars=1,
     )
     wsend, dq_part = lax.optimization_barrier((wsend, dq_part))
-    dkv_keep, *dqs = call(
+    twice = (2 * PAIR, DH)
+    dkv_keep, dq_keep, dq_send = call(
         functools.partial(backward_kernel, 0),
         "backward_near",
         [q, qm, kv, km, *loads, dq_part],
-        [shape((4, *pair))] + [shape((PAIR, DH))] * 4,
+        [shape((8, *pair)), shape(twice, F32), shape(twice)],
         scratch,
         flops=6 * NQ * NK * DH,
     )
-    mine, *far = call(
+    dk_keep, dk_send, dv_keep, dv_send, wkeep, wsend = call(
         core_kernel,
         "core",
-        [dkv_keep, swapped(dkv_send, "c", 2, 1), wkeep, swapped(wsend, "c", 2, 1), *dqs[1:]],
-        [shape(pair, F32)] + [shape(pair)] * 3 + [shape((256, FEATS), F32)] + [shape((PAIR + 512, DH))] * 3,
-    )
-    dkvs = [mine] + [shifted(far[s - 1], "zr", 4, -s) for s in (1, 2, 3)]
-    xs = [shifted(far[3 + s], "x", 4, -s) for s in (1, 2, 3)]
-    xs, dkvs = lax.optimization_barrier((xs, dkvs))
-    dq, wkeep, wsend = call(
+        [dkv_keep, swapped(dkv_send, "c", 2, 1), wkeep, swapped(wsend, "c", 2, 1)],
+        [shape(twice, F32), shape(twice)] * 2 + [shape((512, FEATS), F32), shape((512, FEATS))],
+    )
+    wkeep, wsend, dk, dk_send, dv, dv_send, dq, dq_send = call(
+        middle_kernel,
+        "middle",
+        [wkeep, swapped(wsend, "x", 4, 3)]
+        + [dk_keep, swapped(dk_send, "zr", 4, 1)]
+        + [dv_keep, swapped(dv_send, "zr", 4, 3)]
+        + [dq_keep, swapped(dq_send, "x", 4, 1)],
+        [shape((256, FEATS), F32), shape((256, FEATS))] + [shape(pair, F32), shape(pair)] * 3,
+    )
+    landed = [swapped(wsend, "x", 4, 1), swapped(dq_send, "x", 4, 3)]
+    landed += [swapped(dk_send, "zr", 4, 3), swapped(dv_send, "zr", 4, 1)]
+    wgot, dq_got, dk_got, dv_got = lax.optimization_barrier(landed)
+    wkeep, wsend = call(
         ring_kernel,
         "ring",
-        [dqs[0], far[3], *xs],
-        [shape((PAIR, DH), F32), shape((128, FEATS), F32), shape((128, FEATS))],
+        [wkeep, wgot],
+        [shape((128, FEATS), F32), shape((128, FEATS))],
     )
     wkeep, wsend = call(
         half_kernel,
@@ -432,7 +477,8 @@
     keep, wkeep, send = call(
         total_kernel,
         "total",
-        [*dkvs, dq, wkeep, swapped(wsend, "zr", 4, 1)],
+        [dq, dq_got, dk, dk_got, dv, dv_got]
+        + [wkeep, swapped(wsend, "zr", 4, 1)],
         [shape((PAD, 3 * DH)), shape((COLS, FEATS), F32), shape((3 * PAD + 2 * COLS, DH))],
     )
     dq, dk, dv, dwo = call(

time: 115 us -> 116 us (level)
  starting transfers between devices: 47.2 us -> 54.3 us
  waiting for transfers between devices: 42.9 us -> 38.8 us
  other arithmetic: 4.28 us -> 2.75 us
    ppermute x12 -> x31, starting transfers between devices: 9.51 us -> 45.2 us  [swapped(): return lax.ppermute(value, axis, [(i, i ^ mask) for i in range(size)])]
    ppermute x21 -> x6, starting transfers between devices: 37.7 us -> 9.15 us  [shifted(): lax.ppermute(value, axis, [(i, (i + by) % size) for i in range(size)])]
    ppermute x21 -> x6, waiting for transfers between devices: 25.2 us -> 0.02 us  [shifted(): lax.ppermute(value, axis, [(i, (i + by) % size) for i in range(size)])]
    ppermute x12 -> x31, waiting for transfers between devices: 17.7 us -> 38.8 us  [swapped(): return lax.ppermute(value, axis, [(i, i ^ mask) for i in range(size)])]
    pallas_call x12 -> x13, Pallas kernels: 18.5 us -> 19.1 us  [call(): pl.pallas_call(kernel, in_specs=[SMEM] * scalars + [VMEM] * (len(ins) - s...]
  transfers between devices with their start and end apart: 33 -> 37, of which waited for: 14 -> 16; matrix products, arithmetic and copies ran while one was open for 2% -> 1% of each run, Pallas kernels for 6% -> 6%
where the time goes in v2:
time: 116 us
  starting transfers between devices  54.3 us (47%)
  waiting for transfers between devices  38.8 us (33%)
  Pallas kernels  19.1 us (16%)
  other arithmetic  2.75 us (2%)
    ppermute x31, starting transfers between devices, swapped(): return lax.ppermute(value, axis, [(i, i ^ mask) for i in range(size)])  45.2 us
    ppermute x31, waiting for transfers between devices, swapped(): return lax.ppermute(value, axis, [(i, i ^ mask) for i in range(size)])  38.8 us
    pallas_call x13, Pallas kernels, call(): pl.pallas_call(kernel, in_specs=[SMEM] * scalars + [VMEM] * (len(ins) - s...  19.1 us
    ppermute x6, starting transfers between devices, shifted(): lax.ppermute(value, axis, [(i, (i + by) % size) for i in range(size)])  9.15 us
  transfers between devices with their start and end apart: 37, of which 16 were waited for; matrix products, arithmetic and copies ran while one was open for 1% of the time, Pallas kernels for 6%

profile of v2, /device:TPU:8, one launch (start us, length us, event | category | flops | bytes accessed | tf_op | source)
XLA Modules:
  0.0 116.2 jit_solution(8652232636684135160)
XLA Ops:
  0.6 0.8 convert_bitcast_fusion.ids_ref.refs_5_
  1.4 1.0 pad_maximum_fusion.1.all_ref
  2.6 0.6 pack.1
  3.2 2.0 %collective-permute-start.8 = (bf16[288,128]{1,0:T(8,128)(2,1)S(1)}, bf16[288,128]{1,0:T(8,128)(2,1)S(1)}, u32[]{:S(2)}, u32[]{:S(2)}) collective-permute-start(bf16[288,128]{1,0:T(8,128)(2,1)S(1)} %get-tuple-element.70), channel_id=1, source_target_pairs={{0,32},{32,0},{1,33},{33,1},{2,34},{34,2},{3,35},{35,3},{4,36},{36... | collective-permute-start | bytes 221192 | tf_op jit(solution)/shard_map/ppermute | solution.py:361
  5.2 0.4 collective-permute-start.2
  5.6 2.6 %collective-permute-start.1 = (bf16[136,512]{1,0:T(8,128)(2,1)S(1)}, bf16[136,512]{1,0:T(8,128)(2,1)S(1)}, u32[]{:S(2)}, u32[]{:S(2)}) collective-permute-start(bf16[136,512]{1,0:T(8,128)(2,1)S(1)} %get-tuple-element.71.refs_0_.dy0_ref), channel_id=1, source_target_pairs={{0,2},{1,3},{2,0},{3,1},{4,6},{5,7},{6,4},{7,5},{8,10},{9,11},{10,... | collective-permute-start | bytes 417800 | tf_op jit(solution)/shard_map/ppermute | solution.py:357
  8.2 1.9 %collective-permute-start = (bf16[136,512]{1,0:T(8,128)(2,1)S(1)}, bf16[136,512]{1,0:T(8,128)(2,1)S(1)}, u32[]{:S(2)}, u32[]{:S(2)}) collective-permute-start(bf16[136,512]{1,0:T(8,128)(2,1)S(1)} %get-tuple-element.71.refs_0_.dy0_ref), channel_id=1, source_target_pairs={{0,1},{1,2},{2,3},{3,0},{4,5},{5,6},{6,7},{7,4},{8,9},{9,10},{10,1... | collective-permute-start | bytes 417800 | tf_op jit(solution)/shard_map/ppermute | solution.py:357
  10.1 0.1 constant_dynamic-slice_fusion.3
  10.2 0.1 pad_maximum_fusion.refs_4_.wo_ref
  10.4 3.4 %collective-permute-start.9 = (bf16[288,128]{1,0:T(8,128)(2,1)S(1)}, bf16[288,128]{1,0:T(8,128)(2,1)S(1)}, u32[]{:S(2)}, u32[]{:S(2)}) collective-permute-start(bf16[288,128]{1,0:T(8,128)(2,1)S(1)} %pad_maximum_fusion.8), channel_id=1, source_target_pairs={{0,64},{64,0},{128,192},{192,128},{1,65},{65,1},{129,193},{193,129... | collective-permute-start | bytes 221192 | tf_op jit(solution)/shard_map/ppermute | solution.py:361
  13.8 3.6 %collective-permute-start.11 = (bf16[288,128]{1,0:T(8,128)(2,1)S(1)}, bf16[288,128]{1,0:T(8,128)(2,1)S(1)}, u32[]{:S(2)}, u32[]{:S(2)}) collective-permute-start(bf16[288,128]{1,0:T(8,128)(2,1)S(1)} %pad_maximum_fusion.9), channel_id=1, source_target_pairs={{0,192},{64,128},{128,64},{192,0},{1,193},{65,129},{129,65},{193,1... | collective-permute-start | bytes 221192 | tf_op jit(solution)/shard_map/ppermute | solution.py:361
  17.4 1.0 dattn.1
  18.4 1.1 collective-permute-start.3
  19.5 1.2 %collective-permute-done.11 = bf16[288,128]{1,0:T(8,128)(2,1)S(1)} collective-permute-done((bf16[288,128]{1,0:T(8,128)(2,1)S(1)}, bf16[288,128]{1,0:T(8,128)(2,1)S(1)}, u32[]{:S(2)}, u32[]{:S(2)}) %collective-permute-start.11) | collective-permute-done | bytes 73760 | tf_op jit(solution)/shard_map/ppermute | solution.py:361
  20.7 0.1 collective-permute-start.15
  20.8 1.1 collective-permute-start.12
  22.0 0.2 collective-permute-start.13
  22.2 3.7 %collective-permute-start.10 = (bf16[576,128]{1,0:T(8,128)(2,1)S(1)}, bf16[576,128]{1,0:T(8,128)(2,1)S(1)}, u32[]{:S(2)}, u32[]{:S(2)}) collective-permute-start(bf16[576,128]{1,0:T(8,128)(2,1)S(1)} %pad_maximum_fusion.4.refs_4_), channel_id=1, source_target_pairs={{0,192},{64,128},{128,64},{192,0},{1,193},{65,129},{129,65},{193,1... | collective-permute-start | bytes 442376 | tf_op jit(solution)/shard_map/ppermute | solution.py:361
  25.9 2.8 %collective-permute-start.6 = (bf16[288,128]{1,0:T(8,128)(2,1)S(1)}, bf16[288,128]{1,0:T(8,128)(2,1)S(1)}, u32[]{:S(2)}, u32[]{:S(2)}) collective-permute-start(bf16[288,128]{1,0:T(8,128)(2,1)S(1)} %pad_maximum_fusion.7), channel_id=1, source_target_pairs={{0,24},{8,16},{16,8},{24,0},{1,25},{9,17},{17,9},{25,1},{2,26},{10... | collective-permute-start | bytes 221192 | tf_op jit(solution)/shard_map/ppermute | solution.py:361
  28.8 2.8 %collective-permute-done.6 = bf16[288,128]{1,0:T(8,128)(2,1)S(1)} collective-permute-done((bf16[288,128]{1,0:T(8,128)(2,1)S(1)}, bf16[288,128]{1,0:T(8,128)(2,1)S(1)}, u32[]{:S(2)}, u32[]{:S(2)}) %collective-permute-start.6) | collective-permute-done | bytes 73760 | tf_op jit(solution)/shard_map/ppermute | solution.py:361
  31.6 0.3 collective-permute-start.4
  31.9 4.1 %collective-permute-done.4 = bf16[288,128]{1,0:T(8,128)(2,1)S(1)} collective-permute-done((bf16[288,128]{1,0:T(8,128)(2,1)S(1)}, bf16[288,128]{1,0:T(8,128)(2,1)S(1)}, u32[]{:S(2)}, u32[]{:S(2)}) %collective-permute-start.4) | collective-permute-done | bytes 73760 | tf_op jit(solution)/shard_map/ppermute | solution.py:361
  35.9 0.3 collective-permute-start.7
  36.2 2.6 %collective-permute-start.5 = (bf16[576,128]{1,0:T(8,128)(2,1)S(1)}, bf16[576,128]{1,0:T(8,128)(2,1)S(1)}, u32[]{:S(2)}, u32[]{:S(2)}) collective-permute-start(bf16[576,128]{1,0:T(8,128)(2,1)S(1)} %pad_maximum_fusion.2.refs_0_), channel_id=1, source_target_pairs={{0,24},{8,16},{16,8},{24,0},{1,25},{9,17},{17,9},{25,1},{2,26},{10... | collective-permute-start | bytes 442376 | tf_op jit(solution)/shard_map/ppermute | solution.py:361
  38.8 0.5 collective-permute-start.14
  39.3 1.7 %collective-permute-done.7.refs_3_ = bf16[576,128]{1,0:T(8,128)(2,1)S(1)} collective-permute-done((bf16[576,128]{1,0:T(8,128)(2,1)S(1)}, bf16[576,128]{1,0:T(8,128)(2,1)S(1)}, u32[]{:S(2)}, u32[]{:S(2)}) %collective-permute-start.7) | collective-permute-done | bytes 147488 | tf_op jit(solution)/shard_map/ppermute | solution.py:361
  41.1 1.6 %collective-permute-done.5.refs_1_ = bf16[576,128]{1,0:T(8,128)(2,1)S(1)} collective-permute-done((bf16[576,128]{1,0:T(8,128)(2,1)S(1)}, bf16[576,128]{1,0:T(8,128)(2,1)S(1)}, u32[]{:S(2)}, u32[]{:S(2)}) %collective-permute-start.5) | collective-permute-done | bytes 147488 | tf_op jit(solution)/shard_map/ppermute | solution.py:361
  42.7 5.3 %forward.1 = (bf16[368,128]{1,0:T(8,128)(2,1)S(1)}, bf16[368,128]{1,0:T(8,128)(2,1)S(1)}, bf16[368,128]{1,0:T(8,128)(2,1)S(1)}, bf16[368,128]{1,0:T(8,128)(2,1)S...) custom-call(bf16[576,128]{1,0:T(8,128)(2,1)S(1)} %pad_maximum_fusion, ...), custom_call_target="tpu_custom_call" | custom-call | flops 2038431744 | bytes 1048576 | tf_op jit(solution)/shard_map/forward/pallas_call | solution.py:47
  48.0 0.8 collective-permute-start.17
  48.8 3.3 %collective-permute-start.18 = (bf16[368,128]{1,0:T(8,128)(2,1)S(1)}, bf16[368,128]{1,0:T(8,128)(2,1)S(1)}, u32[]{:S(2)}, u32[]{:S(2)}) collective-permute-start(bf16[368,128]{1,0:T(8,128)(2,1)S(1)} %get-tuple-element.80), channel_id=1, source_target_pairs={{0,16},{8,24},{16,0},{24,8},{1,17},{9,25},{17,1},{25,9},{2,18},{10... | collective-permute-start | bytes 282632 | tf_op jit(solution)/shard_map/ppermute | solution.py:361
  52.0 0.8 collective-permute-start.19
  52.8 2.8 %collective-permute-done.18.l2_ref.refs_2_ = bf16[368,128]{1,0:T(8,128)(2,1)S(1)} collective-permute-done((bf16[368,128]{1,0:T(8,128)(2,1)S(1)}, bf16[368,128]{1,0:T(8,128)(2,1)S(1)}, u32[]{:S(2)}, u32[]{:S(2)}) %collective-permute-start.18) | collective-permute-done | bytes 94240 | tf_op jit(solution)/shard_map/ppermute | solution.py:361
  55.6 2.2 %collective-permute-done.19.l3_ref.refs_3_ = bf16[368,128]{1,0:T(8,128)(2,1)S(1)} collective-permute-done((bf16[368,128]{1,0:T(8,128)(2,1)S(1)}, bf16[368,128]{1,0:T(8,128)(2,1)S(1)}, u32[]{:S(2)}, u32[]{:S(2)}) %collective-permute-start.19) | collective-permute-done | bytes 94240 | tf_op jit(solution)/shard_map/ppermute | solution.py:361
  57.8 0.8 merge.1
  58.7 4.2 %backward_far.1 = (bf16[8,288,128]{2,1,0:T(8,128)(2,1)S(1)}, f32[1152,128]{1,0:T(8,128)S(1)}) custom-call(bf16[1152,256]{1,0:T(8,128)(2,1)S(1)} %get-tuple-element.85.q_ref, bf16[1152,128]{1,0:T(8,128)(2,1)S(1)} %get-tuple-element.86.qm_ref, bf16[2304,256]{1,0:T(8,128)(2,1)S(1)} %get-tuple-element.87.kv_ref, bf16[2304,128]{1,0:T(8,128)(2,1)S(1)} %get-tuple-element.88.km_ref, ...), custom_call_target="tpu_custom_call" | custom-call | flops 2038431744 | bytes 1048576 | tf_op jit(solution)/shard_map/backward_far/pallas_call | solution.py:47
  62.9 0.1 collective-permute-start.24
  63.0 2.0 %collective-permute-start.20 = (bf16[144,128]{1,0:T(8,128)(2,1)S(1)}, bf16[144,128]{1,0:T(8,128)(2,1)S(1)}, u32[]{:S(2)}, u32[]{:S(2)}) collective-permute-start(bf16[144,128]{1,0:T(8,128)(2,1)S(1)} %get-tuple-element.83), channel_id=1, source_target_pairs={{0,32},{32,0},{1,33},{33,1},{2,34},{34,2},{3,35},{35,3},{4,36},{36... | collective-permute-start | bytes 110600 | tf_op jit(solution)/shard_map/ppermute | solution.py:361
  64.9 2.3 %collective-permute-done.20.other_ref = bf16[144,128]{1,0:T(8,128)(2,1)S(1)} collective-permute-done((bf16[144,128]{1,0:T(8,128)(2,1)S(1)}, bf16[144,128]{1,0:T(8,128)(2,1)S(1)}, u32[]{:S(2)}, u32[]{:S(2)}) %collective-permute-start.20) | collective-permute-done | bytes 36896 | tf_op jit(solution)/shard_map/ppermute | solution.py:361
  67.2 1.2 %project.1 = (bf16[136,512]{1,0:T(8,128)(2,1)S(1)}, bf16[136,512]{1,0:T(8,128)(2,1)S(1)}, bf16[136,512]{1,0:T(8,128)(2,1)S(1)}, bf16[136,512]{1,0:T(8,128)(2,1)S...) custom-call(s32[5]{0:T(128)S(1)} %stack.23.at_ref, ...), custom_call_target="tpu_custom_call" | custom-call | tf_op jit(solution)/shard_map/project/pallas_call | solution.py:47
  68.6 4.2 %backward_near.1 = (bf16[8,288,128]{2,1,0:T(8,128)(2,1)S(1)}, f32[576,128]{1,0:T(8,128)S(1)}, bf16[576,128]{1,0:T(8,128)(2,1)S(1)}) custom-call(bf16[1152,256]{1,0:T(8,128)(2,1)S(1)} %get-tuple-element.85.q_ref, bf16[1152,128]{1,0:T(8,128)(2,1)S(1)} %get-tuple-element.86.qm_ref, bf16[2304,256]{1,0:T(8,128)(2,1)S(1)} %get-tuple-element.87.kv_ref, ...), custom_call_target="tpu_custom_call" | custom-call | flops 2038431744 | bytes 1048576 | tf_op jit(solution)/shard_map/backward_near/pallas_call | solution.py:47
  72.8 0.2 core.1
  73.0 0.8 collective-permute-start.26
  73.9 2.1 %collective-permute-start.27 = (bf16[576,128]{1,0:T(8,128)(2,1)S(1)}, bf16[576,128]{1,0:T(8,128)(2,1)S(1)}, u32[]{:S(2)}, u32[]{:S(2)}) collective-permute-start(bf16[576,128]{1,0:T(8,128)(2,1)S(1)} %get-tuple-element.105), channel_id=1, source_target_pairs={{0,64},{64,0},{128,192},{192,128},{1,65},{65,1},{129,193},{193,129... | collective-permute-start | bytes 442376 | tf_op jit(solution)/shard_map/ppermute | solution.py:361
  76.0 0.2 collective-permute-start.28
  76.2 3.6 %collective-permute-done.29.refs_7_ = bf16[576,128]{1,0:T(8,128)(2,1)S(1)} collective-permute-done((bf16[576,128]{1,0:T(8,128)(2,1)S(1)}, bf16[576,128]{1,0:T(8,128)(2,1)S(1)}, u32[]{:S(2)}, u32[]{:S(2)}) %collective-permute-start.29) | collective-permute-done | bytes 147488 | tf_op jit(solution)/shard_map/ppermute | solution.py:361
  79.8 3.3 %collective-permute-done.27.refs_3_ = bf16[576,128]{1,0:T(8,128)(2,1)S(1)} collective-permute-done((bf16[576,128]{1,0:T(8,128)(2,1)S(1)}, bf16[576,128]{1,0:T(8,128)(2,1)S(1)}, u32[]{:S(2)}, u32[]{:S(2)}) %collective-permute-start.27) | collective-permute-done | bytes 147488 | tf_op jit(solution)/shard_map/ppermute | solution.py:361
  83.1 3.6 %collective-permute-done.28.refs_5_ = bf16[576,128]{1,0:T(8,128)(2,1)S(1)} collective-permute-done((bf16[576,128]{1,0:T(8,128)(2,1)S(1)}, bf16[576,128]{1,0:T(8,128)(2,1)S(1)}, u32[]{:S(2)}, u32[]{:S(2)}) %collective-permute-start.28) | collective-permute-done | bytes 147488 | tf_op jit(solution)/shard_map/ppermute | solution.py:361
  86.8 0.1 middle.1
  86.9 1.8 %collective-permute-start.30 = (bf16[256,256]{1,0:T(8,128)(2,1)S(1)}, bf16[256,256]{1,0:T(8,128)(2,1)S(1)}, u32[]{:S(2)}, u32[]{:S(2)}) collective-permute-start(bf16[256,256]{1,0:T(8,128)(2,1)S(1)} %get-tuple-element.111), channel_id=1, source_target_pairs={{0,8},{8,0},{16,24},{24,16},{1,9},{9,1},{17,25},{25,17},{2,10},{10... | collective-permute-start | bytes 393224 | tf_op jit(solution)/shard_map/ppermute | solution.py:361
  88.7 2.5 %collective-permute-start.31 = (bf16[288,128]{1,0:T(8,128)(2,1)S(1)}, bf16[288,128]{1,0:T(8,128)(2,1)S(1)}, u32[]{:S(2)}, u32[]{:S(2)}) collective-permute-start(bf16[288,128]{1,0:T(8,128)(2,1)S(1)} %get-tuple-element.112), channel_id=1, source_target_pairs={{0,24},{8,16},{16,8},{24,0},{1,25},{9,17},{17,9},{25,1},{2,26},{10... | collective-permute-start | bytes 221192 | tf_op jit(solution)/shard_map/ppermute | solution.py:361
  91.2 1.5 %collective-permute-start.33 = (bf16[288,128]{1,0:T(8,128)(2,1)S(1)}, bf16[288,128]{1,0:T(8,128)(2,1)S(1)}, u32[]{:S(2)}, u32[]{:S(2)}) collective-permute-start(bf16[288,128]{1,0:T(8,128)(2,1)S(1)} %get-tuple-element.114), channel_id=1, source_target_pairs={{0,64},{64,0},{128,192},{192,128},{1,65},{65,1},{129,193},{193,129... | collective-permute-start | bytes 221192 | tf_op jit(solution)/shard_map/ppermute | solution.py:361
  92.7 1.0 collective-permute-start.21
  93.7 0.6 collective-permute-done.31.refs_1_
  94.3 2.8 %collective-permute-start.22 = (bf16[136,512]{1,0:T(8,128)(2,1)S(1)}, bf16[136,512]{1,0:T(8,128)(2,1)S(1)}, u32[]{:S(2)}, u32[]{:S(2)}) collective-permute-start(bf16[136,512]{1,0:T(8,128)(2,1)S(1)} %get-tuple-element.93), channel_id=1, source_target_pairs={{0,2},{1,3},{2,0},{3,1},{4,6},{5,7},{6,4},{7,5},{8,10},{9,11},{10,... | collective-permute-start | bytes 417800 | tf_op jit(solution)/shard_map/ppermute | solution.py:357
  97.1 0.8 collective-permute-done.32.refs_3_
  97.9 0.4 collective-permute-start.23
  98.3 2.6 %collective-permute-start.34 = (bf16[128,256]{1,0:T(8,128)(2,1)S(1)}, bf16[128,256]{1,0:T(8,128)(2,1)S(1)}, u32[]{:S(2)}, u32[]{:S(2)}) collective-permute-start(bf16[128,256]{1,0:T(8,128)(2,1)S(1)} %get-tuple-element.123), channel_id=1, source_target_pairs={{0,192},{64,128},{128,64},{192,0},{1,193},{65,129},{129,65},{193,1... | collective-permute-start | bytes 196616 | tf_op jit(solution)/shard_map/ppermute | solution.py:361
  100.9 3.8 %collective-permute-done.34.got_ref = bf16[128,256]{1,0:T(8,128)(2,1)S(1)} collective-permute-done((bf16[128,256]{1,0:T(8,128)(2,1)S(1)}, bf16[128,256]{1,0:T(8,128)(2,1)S(1)}, u32[]{:S(2)}, u32[]{:S(2)}) %collective-permute-start.34) | collective-permute-done | bytes 65568 | tf_op jit(solution)/shard_map/ppermute | solution.py:361
  104.8 2.8 %collective-permute-start.35 = (bf16[64,256]{1,0:T(8,128)(2,1)S(1)}, bf16[64,256]{1,0:T(8,128)(2,1)S(1)}, u32[]{:S(2)}, u32[]{:S(2)}) collective-permute-start(bf16[64,256]{1,0:T(8,128)(2,1)S(1)} %get-tuple-element.125), channel_id=1, source_target_pairs={{0,64},{64,0},{128,192},{192,128},{1,65},{65,1},{129,193},{193,129... | collective-permute-start | bytes 98312 | tf_op jit(solution)/shard_map/ppermute | solution.py:361
  107.6 2.2 %collective-permute-done.35.refs_7_ = bf16[64,256]{1,0:T(8,128)(2,1)S(1)} collective-permute-done((bf16[64,256]{1,0:T(8,128)(2,1)S(1)}, bf16[64,256]{1,0:T(8,128)(2,1)S(1)}, u32[]{:S(2)}, u32[]{:S(2)}) %collective-permute-start.35) | collective-permute-done | bytes 32800 | tf_op jit(solution)/shard_map/ppermute | solution.py:361
  109.8 2.2 %collective-permute-start.36 = (bf16[496,128]{1,0:T(8,128)(2,1)S(1)}, bf16[496,128]{1,0:T(8,128)(2,1)S(1)}, u32[]{:S(2)}, u32[]{:S(2)}) collective-permute-start(bf16[496,128]{1,0:T(8,128)(2,1)S(1)} %get-tuple-element.128), channel_id=1, source_target_pairs={{0,32},{32,0},{1,33},{33,1},{2,34},{34,2},{3,35},{35,3},{4,36},{36... | collective-permute-start | bytes 380936 | tf_op jit(solution)/shard_map/ppermute | solution.py:361
  112.0 0.7 add_convert_fusion
  112.7 2.2 %collective-permute-done.36.got_ref = bf16[496,128]{1,0:T(8,128)(2,1)S(1)} collective-permute-done((bf16[496,128]{1,0:T(8,128)(2,1)S(1)}, bf16[496,128]{1,0:T(8,128)(2,1)S(1)}, u32[]{:S(2)}, u32[]{:S(2)}) %collective-permute-start.36) | collective-permute-done | bytes 127008 | tf_op jit(solution)/shard_map/ppermute | solution.py:361
  114.9 1.3 %place.1 = (bf16[136,256]{1,0:T(8,128)(2,1)}, bf16[136,256]{1,0:T(8,128)(2,1)}, bf16[136,256]{1,0:T(8,128)(2,1)}, f32[32,256]{1,0:T(8,128)}) custom-call(s32[5]{0:T(128)S(1)} %stack.23.at_ref, bf16[144,384]{1,0:T(8,128)(2,1)S(1)} %get-tuple-element.126.mine_ref, f32[32,256]{1,0:T(8,128)S(1)} %get-tuple-element.127.wmine_ref, ...), custom_call_target="tpu_custom_call" | custom-call | tf_op jit(solution)/shard_map/place/pallas_call | solution.py:47
  (43 shorter events, 0.4 us)
Async XLA Ops:
  0.6 9.5 %copy-start = (bf16[256,2048]{1,0:T(8,128)(2,1)S(1)}, bf16[256,2048]{1,0:T(8,128)(2,1)}, u32[]{:S(2)}) copy-start(bf16[256,2048]{1,0:T(8,128)(2,1)} %param.10) | copy-start | bytes 3145732
  3.2 7.2 %collective-permute-start.8 = (bf16[288,128]{1,0:T(8,128)(2,1)S(1)}, bf16[288,128]{1,0:T(8,128)(2,1)S(1)}, u32[]{:S(2)}, u32[]{:S(2)}) collective-permute-start(bf16[288,128]{1,0:T(8,128)(2,1)S(1)} %get-tuple-element.70), channel_id=1, source_target_pairs={{0,32},{32,0},{1,33},{33,1},{2,34},{34,2},{3,35},{35,3},{4,36},{36... | collective-permute-start | bytes 221192 | tf_op jit(solution)/shard_map/ppermute | solution.py:361
  5.2 12.2 %collective-permute-start.2 = (bf16[136,512]{1,0:T(8,128)(2,1)S(1)}, bf16[136,512]{1,0:T(8,128)(2,1)S(1)}, u32[]{:S(2)}, u32[]{:S(2)}) collective-permute-start(bf16[136,512]{1,0:T(8,128)(2,1)S(1)} %get-tuple-element.71.refs_0_.dy0_ref), channel_id=1, source_target_pairs={{0,3},{1,0},{2,1},{3,2},{4,7},{5,4},{6,5},{7,6},{8,11},{9,8},{10,9... | collective-permute-start | bytes 417800 | tf_op jit(solution)/shard_map/ppermute | solution.py:357
  5.6 11.7 %collective-permute-start.1 = (bf16[136,512]{1,0:T(8,128)(2,1)S(1)}, bf16[136,512]{1,0:T(8,128)(2,1)S(1)}, u32[]{:S(2)}, u32[]{:S(2)}) collective-permute-start(bf16[136,512]{1,0:T(8,128)(2,1)S(1)} %get-tuple-element.71.refs_0_.dy0_ref), channel_id=1, source_target_pairs={{0,2},{1,3},{2,0},{3,1},{4,6},{5,7},{6,4},{7,5},{8,10},{9,11},{10,... | collective-permute-start | bytes 417800 | tf_op jit(solution)/shard_map/ppermute | solution.py:357
  8.2 9.1 %collective-permute-start = (bf16[136,512]{1,0:T(8,128)(2,1)S(1)}, bf16[136,512]{1,0:T(8,128)(2,1)S(1)}, u32[]{:S(2)}, u32[]{:S(2)}) collective-permute-start(bf16[136,512]{1,0:T(8,128)(2,1)S(1)} %get-tuple-element.71.refs_0_.dy0_ref), channel_id=1, source_target_pairs={{0,1},{1,2},{2,3},{3,0},{4,5},{5,6},{6,7},{7,4},{8,9},{9,10},{10,1... | collective-permute-start | bytes 417800 | tf_op jit(solution)/shard_map/ppermute | solution.py:357
  10.4 11.5 %collective-permute-start.9 = (bf16[288,128]{1,0:T(8,128)(2,1)S(1)}, bf16[288,128]{1,0:T(8,128)(2,1)S(1)}, u32[]{:S(2)}, u32[]{:S(2)}) collective-permute-start(bf16[288,128]{1,0:T(8,128)(2,1)S(1)} %pad_maximum_fusion.8), channel_id=1, source_target_pairs={{0,64},{64,0},{128,192},{192,128},{1,65},{65,1},{129,193},{193,129... | collective-permute-start | bytes 221192 | tf_op jit(solution)/shard_map/ppermute | solution.py:361
  13.8 6.9 %collective-permute-start.11 = (bf16[288,128]{1,0:T(8,128)(2,1)S(1)}, bf16[288,128]{1,0:T(8,128)(2,1)S(1)}, u32[]{:S(2)}, u32[]{:S(2)}) collective-permute-start(bf16[288,128]{1,0:T(8,128)(2,1)S(1)} %pad_maximum_fusion.9), channel_id=1, source_target_pairs={{0,192},{64,128},{128,64},{192,0},{1,193},{65,129},{129,65},{193,1... | collective-permute-start | bytes 221192 | tf_op jit(solution)/shard_map/ppermute | solution.py:361
  18.4 7.5 %collective-permute-start.3 = (bf16[288,128]{1,0:T(8,128)(2,1)S(1)}, bf16[288,128]{1,0:T(8,128)(2,1)S(1)}, u32[]{:S(2)}, u32[]{:S(2)}) collective-permute-start(bf16[288,128]{1,0:T(8,128)(2,1)S(1)} %get-tuple-element.76), channel_id=1, source_target_pairs={{0,32},{32,0},{1,33},{33,1},{2,34},{34,2},{3,35},{35,3},{4,36},{36... | collective-permute-start | bytes 221192 | tf_op jit(solution)/shard_map/ppermute | solution.py:361
  20.7 15.5 %collective-permute-start.15 = (bf16[576,128]{1,0:T(8,128)(2,1)S(1)}, bf16[576,128]{1,0:T(8,128)(2,1)S(1)}, u32[]{:S(2)}, u32[]{:S(2)}) collective-permute-start(bf16[576,128]{1,0:T(8,128)(2,1)S(1)} %pad_maximum_fusion.5.refs_6_), channel_id=1, source_target_pairs={{0,4},{4,0},{1,5},{5,1},{2,6},{6,2},{3,7},{7,3},{8,12},{12,8},{9,1... | collective-permute-start | bytes 442376 | tf_op jit(solution)/shard_map/ppermute | solution.py:361
  20.8 18.0 %collective-permute-start.12 = (bf16[576,128]{1,0:T(8,128)(2,1)S(1)}, bf16[576,128]{1,0:T(8,128)(2,1)S(1)}, u32[]{:S(2)}, u32[]{:S(2)}) collective-permute-start(bf16[576,128]{1,0:T(8,128)(2,1)S(1)} %pad_maximum_fusion.5.refs_6_), channel_id=1, source_target_pairs={{0,64},{64,0},{128,192},{192,128},{1,65},{65,1},{129,193},{193,129... | collective-permute-start | bytes 442376 | tf_op jit(solution)/shard_map/ppermute | solution.py:361
  22.0 17.4 %collective-permute-start.13 = (bf16[576,128]{1,0:T(8,128)(2,1)S(1)}, bf16[576,128]{1,0:T(8,128)(2,1)S(1)}, u32[]{:S(2)}, u32[]{:S(2)}) collective-permute-start(bf16[576,128]{1,0:T(8,128)(2,1)S(1)} %pad_maximum_fusion.4.refs_4_), channel_id=1, source_target_pairs={{0,4},{4,0},{1,5},{5,1},{2,6},{6,2},{3,7},{7,3},{8,12},{12,8},{9,1... | collective-permute-start | bytes 442376 | tf_op jit(solution)/shard_map/ppermute | solution.py:361
  22.2 16.6 %collective-permute-start.10 = (bf16[576,128]{1,0:T(8,128)(2,1)S(1)}, bf16[576,128]{1,0:T(8,128)(2,1)S(1)}, u32[]{:S(2)}, u32[]{:S(2)}) collective-permute-start(bf16[576,128]{1,0:T(8,128)(2,1)S(1)} %pad_maximum_fusion.4.refs_4_), channel_id=1, source_target_pairs={{0,192},{64,128},{128,64},{192,0},{1,193},{65,129},{129,65},{193,1... | collective-permute-start | bytes 442376 | tf_op jit(solution)/shard_map/ppermute | solution.py:361
  25.9 5.7 %collective-permute-start.6 = (bf16[288,128]{1,0:T(8,128)(2,1)S(1)}, bf16[288,128]{1,0:T(8,128)(2,1)S(1)}, u32[]{:S(2)}, u32[]{:S(2)}) collective-permute-start(bf16[288,128]{1,0:T(8,128)(2,1)S(1)} %pad_maximum_fusion.7), channel_id=1, source_target_pairs={{0,24},{8,16},{16,8},{24,0},{1,25},{9,17},{17,9},{25,1},{2,26},{10... | collective-permute-start | bytes 221192 | tf_op jit(solution)/shard_map/ppermute | solution.py:361
  31.6 4.4 %collective-permute-start.4 = (bf16[288,128]{1,0:T(8,128)(2,1)S(1)}, bf16[288,128]{1,0:T(8,128)(2,1)S(1)}, u32[]{:S(2)}, u32[]{:S(2)}) collective-permute-start(bf16[288,128]{1,0:T(8,128)(2,1)S(1)} %pad_maximum_fusion.6), channel_id=1, source_target_pairs={{0,8},{8,0},{16,24},{24,16},{1,9},{9,1},{17,25},{25,17},{2,10},{10... | collective-permute-start | bytes 221192 | tf_op jit(solution)/shard_map/ppermute | solution.py:361
  35.9 5.1 %collective-permute-start.7 = (bf16[576,128]{1,0:T(8,128)(2,1)S(1)}, bf16[576,128]{1,0:T(8,128)(2,1)S(1)}, u32[]{:S(2)}, u32[]{:S(2)}) collective-permute-start(bf16[576,128]{1,0:T(8,128)(2,1)S(1)} %pad_maximum_fusion.3.refs_2_), channel_id=1, source_target_pairs={{0,8},{8,0},{16,24},{24,16},{1,9},{9,1},{17,25},{25,17},{2,10},{10... | collective-permute-start | bytes 442376 | tf_op jit(solution)/shard_map/ppermute | solution.py:361
  36.2 6.4 %collective-permute-start.5 = (bf16[576,128]{1,0:T(8,128)(2,1)S(1)}, bf16[576,128]{1,0:T(8,128)(2,1)S(1)}, u32[]{:S(2)}, u32[]{:S(2)}) collective-permute-start(bf16[576,128]{1,0:T(8,128)(2,1)S(1)} %pad_maximum_fusion.2.refs_0_), channel_id=1, source_target_pairs={{0,24},{8,16},{16,8},{24,0},{1,25},{9,17},{17,9},{25,1},{2,26},{10... | collective-permute-start | bytes 442376 | tf_op jit(solution)/shard_map/ppermute | solution.py:361
  38.8 3.9 %collective-permute-start.16 = (bf16[576,128]{1,0:T(8,128)(2,1)S(1)}, bf16[576,128]{1,0:T(8,128)(2,1)S(1)}, u32[]{:S(2)}, u32[]{:S(2)}) collective-permute-start(bf16[576,128]{1,0:T(8,128)(2,1)S(1)} %collective-permute-done.12.refs_7_), channel_id=1, source_target_pairs={{0,4},{4,0},{1,5},{5,1},{2,6},{6,2},{3,7},{7,3},{8,12},{12,8},{9,1... | collective-permute-start | bytes 442376 | tf_op jit(solution)/shard_map/ppermute | solution.py:361
  38.8 3.9 %collective-permute-start.14 = (bf16[576,128]{1,0:T(8,128)(2,1)S(1)}, bf16[576,128]{1,0:T(8,128)(2,1)S(1)}, u32[]{:S(2)}, u32[]{:S(2)}) collective-permute-start(bf16[576,128]{1,0:T(8,128)(2,1)S(1)} %collective-permute-done.10.refs_5_), channel_id=1, source_target_pairs={{0,4},{4,0},{1,5},{5,1},{2,6},{6,2},{3,7},{7,3},{8,12},{12,8},{9,1... | collective-permute-start | bytes 442376 | tf_op jit(solution)/shard_map/ppermute | solution.py:361
  48.0 4.8 %collective-permute-start.17 = (bf16[368,128]{1,0:T(8,128)(2,1)S(1)}, bf16[368,128]{1,0:T(8,128)(2,1)S(1)}, u32[]{:S(2)}, u32[]{:S(2)}) collective-permute-start(bf16[368,128]{1,0:T(8,128)(2,1)S(1)} %get-tuple-element.79), channel_id=1, source_target_pairs={{0,8},{8,0},{16,24},{24,16},{1,9},{9,1},{17,25},{25,17},{2,10},{10... | collective-permute-start | bytes 282632 | tf_op jit(solution)/shard_map/ppermute | solution.py:361
  48.8 6.8 %collective-permute-start.18 = (bf16[368,128]{1,0:T(8,128)(2,1)S(1)}, bf16[368,128]{1,0:T(8,128)(2,1)S(1)}, u32[]{:S(2)}, u32[]{:S(2)}) collective-permute-start(bf16[368,128]{1,0:T(8,128)(2,1)S(1)} %get-tuple-element.80), channel_id=1, source_target_pairs={{0,16},{8,24},{16,0},{24,8},{1,17},{9,25},{17,1},{25,9},{2,18},{10... | collective-permute-start | bytes 282632 | tf_op jit(solution)/shard_map/ppermute | solution.py:361
  52.0 5.8 %collective-permute-start.19 = (bf16[368,128]{1,0:T(8,128)(2,1)S(1)}, bf16[368,128]{1,0:T(8,128)(2,1)S(1)}, u32[]{:S(2)}, u32[]{:S(2)}) collective-permute-start(bf16[368,128]{1,0:T(8,128)(2,1)S(1)} %get-tuple-element.81), channel_id=1, source_target_pairs={{0,24},{8,16},{16,8},{24,0},{1,25},{9,17},{17,9},{25,1},{2,26},{10... | collective-permute-start | bytes 282632 | tf_op jit(solution)/shard_map/ppermute | solution.py:361
  62.9 9.9 %collective-permute-start.24 = (bf16[8,288,128]{2,1,0:T(8,128)(2,1)S(1)}, bf16[8,288,128]{2,1,0:T(8,128)(2,1)S(1)}, u32[]{:S(2)}, u32[]{:S(2)}) collective-permute-start(bf16[8,288,128]{2,1,0:T(8,128)(2,1)S(1)} %get-tuple-element.99), channel_id=1, source_target_pairs={{0,4},{4,0},{1,5},{5,1},{2,6},{6,2},{3,7},{7,3},{8,12},{12,8},{9,1... | collective-permute-start | bytes 1769480 | tf_op jit(solution)/shard_map/ppermute | solution.py:361
  63.0 4.3 %collective-permute-start.20 = (bf16[144,128]{1,0:T(8,128)(2,1)S(1)}, bf16[144,128]{1,0:T(8,128)(2,1)S(1)}, u32[]{:S(2)}, u32[]{:S(2)}) collective-permute-start(bf16[144,128]{1,0:T(8,128)(2,1)S(1)} %get-tuple-element.83), channel_id=1, source_target_pairs={{0,32},{32,0},{1,33},{33,1},{2,34},{34,2},{3,35},{35,3},{4,36},{36... | collective-permute-start | bytes 110600 | tf_op jit(solution)/shard_map/ppermute | solution.py:361
  68.5 4.3 %collective-permute-start.25 = (bf16[4,256,256]{2,1,0:T(8,128)(2,1)S(1)}, bf16[4,256,256]{2,1,0:T(8,128)(2,1)S(1)}, u32[]{:S(2)}, u32[]{:S(2)}) collective-permute-start(bf16[4,256,256]{2,1,0:T(8,128)(2,1)S(1)} %get-tuple-element.101), channel_id=1, source_target_pairs={{0,4},{4,0},{1,5},{5,1},{2,6},{6,2},{3,7},{7,3},{8,12},{12,8},{9,1... | collective-permute-start | bytes 1572872 | tf_op jit(solution)/shard_map/ppermute | solution.py:361
  73.0 13.7 %collective-permute-start.26 = (bf16[512,256]{1,0:T(8,128)(2,1)S(1)}, bf16[512,256]{1,0:T(8,128)(2,1)S(1)}, u32[]{:S(2)}, u32[]{:S(2)}) collective-permute-start(bf16[512,256]{1,0:T(8,128)(2,1)S(1)} %get-tuple-element.103), channel_id=1, source_target_pairs={{0,24},{8,16},{16,8},{24,0},{1,25},{9,17},{17,9},{25,1},{2,26},{10... | collective-permute-start | bytes 786440 | tf_op jit(solution)/shard_map/ppermute | solution.py:361
  73.9 6.0 %collective-permute-start.29 = (bf16[576,128]{1,0:T(8,128)(2,1)S(1)}, bf16[576,128]{1,0:T(8,128)(2,1)S(1)}, u32[]{:S(2)}, u32[]{:S(2)}) collective-permute-start(bf16[576,128]{1,0:T(8,128)(2,1)S(1)} %get-tuple-element.109), channel_id=1, source_target_pairs={{0,8},{8,0},{16,24},{24,16},{1,9},{9,1},{17,25},{25,17},{2,10},{10... | collective-permute-start | bytes 442376 | tf_op jit(solution)/shard_map/ppermute | solution.py:361
  73.9 9.3 %collective-permute-start.27 = (bf16[576,128]{1,0:T(8,128)(2,1)S(1)}, bf16[576,128]{1,0:T(8,128)(2,1)S(1)}, u32[]{:S(2)}, u32[]{:S(2)}) collective-permute-start(bf16[576,128]{1,0:T(8,128)(2,1)S(1)} %get-tuple-element.105), channel_id=1, source_target_pairs={{0,64},{64,0},{128,192},{192,128},{1,65},{65,1},{129,193},{193,129... | collective-permute-start | bytes 442376 | tf_op jit(solution)/shard_map/ppermute | solution.py:361
  76.0 10.8 %collective-permute-start.28 = (bf16[576,128]{1,0:T(8,128)(2,1)S(1)}, bf16[576,128]{1,0:T(8,128)(2,1)S(1)}, u32[]{:S(2)}, u32[]{:S(2)}) collective-permute-start(bf16[576,128]{1,0:T(8,128)(2,1)S(1)} %get-tuple-element.107), channel_id=1, source_target_pairs={{0,192},{64,128},{128,64},{192,0},{1,193},{65,129},{129,65},{193,1... | collective-permute-start | bytes 442376 | tf_op jit(solution)/shard_map/ppermute | solution.py:361
  86.9 11.4 %collective-permute-start.30 = (bf16[256,256]{1,0:T(8,128)(2,1)S(1)}, bf16[256,256]{1,0:T(8,128)(2,1)S(1)}, u32[]{:S(2)}, u32[]{:S(2)}) collective-permute-start(bf16[256,256]{1,0:T(8,128)(2,1)S(1)} %get-tuple-element.111), channel_id=1, source_target_pairs={{0,8},{8,0},{16,24},{24,16},{1,9},{9,1},{17,25},{25,17},{2,10},{10... | collective-permute-start | bytes 393224 | tf_op jit(solution)/shard_map/ppermute | solution.py:361
  88.7 5.6 %collective-permute-start.31 = (bf16[288,128]{1,0:T(8,128)(2,1)S(1)}, bf16[288,128]{1,0:T(8,128)(2,1)S(1)}, u32[]{:S(2)}, u32[]{:S(2)}) collective-permute-start(bf16[288,128]{1,0:T(8,128)(2,1)S(1)} %get-tuple-element.112), channel_id=1, source_target_pairs={{0,24},{8,16},{16,8},{24,0},{1,25},{9,17},{17,9},{25,1},{2,26},{10... | collective-permute-start | bytes 221192 | tf_op jit(solution)/shard_map/ppermute | solution.py:361
  91.2 6.7 %collective-permute-start.32 = (bf16[288,128]{1,0:T(8,128)(2,1)S(1)}, bf16[288,128]{1,0:T(8,128)(2,1)S(1)}, u32[]{:S(2)}, u32[]{:S(2)}) collective-permute-start(bf16[288,128]{1,0:T(8,128)(2,1)S(1)} %get-tuple-element.113), channel_id=1, source_target_pairs={{0,192},{64,128},{128,64},{192,0},{1,193},{65,129},{129,65},{193,1... | collective-permute-start | bytes 221192 | tf_op jit(solution)/shard_map/ppermute | solution.py:361
  91.2 7.0 %collective-permute-start.33 = (bf16[288,128]{1,0:T(8,128)(2,1)S(1)}, bf16[288,128]{1,0:T(8,128)(2,1)S(1)}, u32[]{:S(2)}, u32[]{:S(2)}) collective-permute-start(bf16[288,128]{1,0:T(8,128)(2,1)S(1)} %get-tuple-element.114), channel_id=1, source_target_pairs={{0,64},{64,0},{128,192},{192,128},{1,65},{65,1},{129,193},{193,129... | collective-permute-start | bytes 221192 | tf_op jit(solution)/shard_map/ppermute | solution.py:361
  92.7 19.3 %collective-permute-start.21 = (bf16[136,512]{1,0:T(8,128)(2,1)S(1)}, bf16[136,512]{1,0:T(8,128)(2,1)S(1)}, u32[]{:S(2)}, u32[]{:S(2)}) collective-permute-start(bf16[136,512]{1,0:T(8,128)(2,1)S(1)} %get-tuple-element.92), channel_id=1, source_target_pairs={{0,1},{1,2},{2,3},{3,0},{4,5},{5,6},{6,7},{7,4},{8,9},{9,10},{10,1... | collective-permute-start | bytes 417800 | tf_op jit(solution)/shard_map/ppermute | solution.py:357
  94.3 17.7 %collective-permute-start.22 = (bf16[136,512]{1,0:T(8,128)(2,1)S(1)}, bf16[136,512]{1,0:T(8,128)(2,1)S(1)}, u32[]{:S(2)}, u32[]{:S(2)}) collective-permute-start(bf16[136,512]{1,0:T(8,128)(2,1)S(1)} %get-tuple-element.93), channel_id=1, source_target_pairs={{0,2},{1,3},{2,0},{3,1},{4,6},{5,7},{6,4},{7,5},{8,10},{9,11},{10,... | collective-permute-start | bytes 417800 | tf_op jit(solution)/shard_map/ppermute | solution.py:357
  97.9 14.1 %collective-permute-start.23 = (bf16[136,512]{1,0:T(8,128)(2,1)S(1)}, bf16[136,512]{1,0:T(8,128)(2,1)S(1)}, u32[]{:S(2)}, u32[]{:S(2)}) collective-permute-start(bf16[136,512]{1,0:T(8,128)(2,1)S(1)} %get-tuple-element.94), channel_id=1, source_target_pairs={{0,3},{1,0},{2,1},{3,2},{4,7},{5,4},{6,5},{7,6},{8,11},{9,8},{10,9... | collective-permute-start | bytes 417800 | tf_op jit(solution)/shard_map/ppermute | solution.py:357
  98.3 6.5 %collective-permute-start.34 = (bf16[128,256]{1,0:T(8,128)(2,1)S(1)}, bf16[128,256]{1,0:T(8,128)(2,1)S(1)}, u32[]{:S(2)}, u32[]{:S(2)}) collective-permute-start(bf16[128,256]{1,0:T(8,128)(2,1)S(1)} %get-tuple-element.123), channel_id=1, source_target_pairs={{0,192},{64,128},{128,64},{192,0},{1,193},{65,129},{129,65},{193,1... | collective-permute-start | bytes 196616 | tf_op jit(solution)/shard_map/ppermute | solution.py:361
  104.8 5.0 %collective-permute-start.35 = (bf16[64,256]{1,0:T(8,128)(2,1)S(1)}, bf16[64,256]{1,0:T(8,128)(2,1)S(1)}, u32[]{:S(2)}, u32[]{:S(2)}) collective-permute-start(bf16[64,256]{1,0:T(8,128)(2,1)S(1)} %get-tuple-element.125), channel_id=1, source_target_pairs={{0,64},{64,0},{128,192},{192,128},{1,65},{65,1},{129,193},{193,129... | collective-permute-start | bytes 98312 | tf_op jit(solution)/shard_map/ppermute | solution.py:361
  109.8 5.1 %collective-permute-start.36 = (bf16[496,128]{1,0:T(8,128)(2,1)S(1)}, bf16[496,128]{1,0:T(8,128)(2,1)S(1)}, u32[]{:S(2)}, u32[]{:S(2)}) collective-permute-start(bf16[496,128]{1,0:T(8,128)(2,1)S(1)} %get-tuple-element.128), channel_id=1, source_target_pairs={{0,32},{32,0},{1,33},{33,1},{2,34},{34,2},{3,35},{35,3},{4,36},{36... | collective-permute-start | bytes 380936 | tf_op jit(solution)/shard_map/ppermute | solution.py:361
